TPU v7x, 32 devices: a whole 2x2x4 slice. The times are simulated.
32 devices in a mesh: mem: 8 (over z, x), fsdp: 4 (over y, core).
Axes of the slice: x: 2, y: 2, z: 4, core: 2. Of those that a mesh axis runs over, the one named last changes fastest.
Arguments:
- queries: bfloat16 [8192, 1024], P(('mem', 'fsdp')), may hold values from -10 to 10
- keys: bfloat16 [8192, 1024], P(('mem', 'fsdp')), may hold values from -7 to 7
- values: bfloat16 [8192, 1024], P(('mem', 'fsdp')), may hold values from -6 to 6
- mem_keys: bfloat16 [32768, 1024], P('mem', 'fsdp'), may hold values from -7 to 7
- mem_values: bfloat16 [32768, 1024], P('mem', 'fsdp'), may hold values from -6 to 6
- block_ids: int32 [16, 4, 8], replicated, may hold values from 0 to 255, as said below
- gate_bias: float32 [16], replicated, may hold values from -2 to 2
- out_weight: bfloat16 [1024, 2048], P('fsdp'), may hold values from -0.59765625 to 0.59765625
- cotangent: bfloat16 [8192, 2048], P(('mem', 'fsdp')), may hold values from -6 to 6
Outputs:
- projected: bfloat16 [8192, 2048], P(('mem', 'fsdp'))
- query_grad: bfloat16 [8192, 1024], P(('mem', 'fsdp'))
- key_grad: bfloat16 [8192, 1024], P(('mem', 'fsdp'))
- value_grad: bfloat16 [8192, 1024], P(('mem', 'fsdp'))
- weight_grad: float32 [1024, 2048], P('fsdp', 'mem')
Inputs may be any that keep to these rules, and one draw needn't show every extreme that they name: `block_ids`: within one segment the 32 ids are distinct, at most 8 of them lie in the blocks of one index of mem (id // 32), and some index of mem has exactly 8 of them in every segment.
All inputs are finite; a program needn't handle non-finite values.
Results may differ from a plain program's by a relative error of at most 0.022.
Values may be sent and summed in bfloat16 or wider, within the bound.
No kernel may reach another device: no remote copies, remote signals or barrier semaphores. Data moves between devices by JAX's collectives and lax.ppermute only.
A program may use at most 192 MiB of HBM per device.

v0:
```python
import jax
import jax.numpy as jnp
from jax import lax
from jax.sharding import PartitionSpec as P

DH = 64
SEG_LEN = 512
QBLK = 128
MBLK = 128
RETR = 8
SEG_DEV = 2
MB_DEV = 32


def softmax_rows(scores):
    largest = jnp.max(scores, axis=-1, keepdims=True)
    weights = jnp.exp(scores - largest)
    return weights / jnp.sum(weights, axis=-1, keepdims=True)


def rounded(array):
    return array.astype(jnp.bfloat16)


def per_device(
    queries, keys, values, mem_keys, mem_values, block_ids, gate_bias, out_weight, cotangent
):
    quarter_width = mem_keys.shape[1]
    heads_here = quarter_width // DH
    mem_count = lax.axis_size("mem")
    owner_index = lax.axis_index("mem")
    scaling = DH ** (-0.5)
    blocks_per_segment = SEG_LEN // QBLK
    capacity = 2 * max(1, RETR * blocks_per_segment // mem_count)
    gating = jax.nn.sigmoid(
        lax.dynamic_slice_in_dim(gate_bias, lax.axis_index("fsdp") * heads_here, heads_here)
    )
    local_share = 1.0 - gating
    row_total = SEG_DEV * SEG_LEN
    head_shape = (SEG_DEV, SEG_LEN, heads_here, DH)
    query_rows, key_rows, value_rows = (
        lax.all_to_all(queries, "fsdp", split_axis=1, concat_axis=0, tiled=True),
        lax.all_to_all(keys, "fsdp", split_axis=1, concat_axis=0, tiled=True),
        lax.all_to_all(values, "fsdp", split_axis=1, concat_axis=0, tiled=True),
    )
    query_heads = query_rows.reshape(head_shape)
    key_heads = key_rows.reshape(head_shape)
    value_heads = value_rows.reshape(head_shape)
    segment_total = block_ids.shape[0]
    request_count = blocks_per_segment * RETR
    flat_ids = block_ids.reshape(segment_total, request_count)
    owners = flat_ids // MB_DEV
    local_block = flat_ids - owners * MB_DEV
    positions = jnp.arange(request_count, dtype=jnp.int32)
    before = positions[None, :] < positions[:, None]
    same_owner = owners[:, :, None] == owners[:, None, :]
    ranking = jnp.sum(jnp.logical_and(same_owner, before[None]), axis=-1)
    matches = jnp.logical_and(
        (owners == owner_index)[:, :, None],
        ranking[:, :, None] == jnp.arange(capacity, dtype=jnp.int32)[None, None, :],
    )
    wanted = jnp.sum(jnp.where(matches, local_block[:, :, None], 0), axis=1)
    wanted = wanted.reshape(mem_count, SEG_DEV, capacity)
    key_store = mem_keys.reshape(MB_DEV, MBLK, quarter_width)
    value_store = mem_values.reshape(MB_DEV, MBLK, quarter_width)
    send_keys = jnp.take(key_store, wanted, axis=0)
    send_values = jnp.take(value_store, wanted, axis=0)
    got_keys, got_values = (
        lax.all_to_all(send_keys, "mem", split_axis=0, concat_axis=0, tiled=True),
        lax.all_to_all(send_values, "mem", split_axis=0, concat_axis=0, tiled=True),
    )
    my_owners = lax.dynamic_slice_in_dim(owners, owner_index * SEG_DEV, SEG_DEV, 0)
    my_ranking = lax.dynamic_slice_in_dim(ranking, owner_index * SEG_DEV, SEG_DEV, 0)
    segment_pos = jnp.arange(SEG_DEV, dtype=jnp.int32)[:, None]
    slot_index = ((my_owners * SEG_DEV + segment_pos) * capacity + my_ranking).reshape(-1)
    flat_keys = got_keys.reshape(mem_count * SEG_DEV * capacity, MBLK, quarter_width)
    flat_values = got_values.reshape(mem_count * SEG_DEV * capacity, MBLK, quarter_width)
    block_shape = (SEG_DEV, blocks_per_segment, RETR * MBLK, heads_here, DH)
    fetched_keys = jnp.take(flat_keys, slot_index, axis=0).reshape(block_shape)
    fetched_values = jnp.take(flat_values, slot_index, axis=0).reshape(block_shape)
    causal = jnp.arange(SEG_LEN)[None, :] <= jnp.arange(SEG_LEN)[:, None]
    local_scores = (
        jnp.einsum("sqhd,skhd->shqk", query_heads, key_heads, preferred_element_type=jnp.float32)
        * scaling
    )
    local_scores = jnp.where(causal[None, None], local_scores, -1e30)
    local_weights = softmax_rows(local_scores)
    local_rounded = rounded(local_weights)
    local_result = jnp.einsum(
        "shqk,skhd->sqhd", local_rounded, value_heads, preferred_element_type=jnp.float32
    )
    query_blocks = query_heads.reshape(SEG_DEV, blocks_per_segment, QBLK, heads_here, DH)
    memory_scores = (
        jnp.einsum(
            "sbqhd,sbkhd->sbhqk", query_blocks, fetched_keys, preferred_element_type=jnp.float32
        )
        * scaling
    )
    memory_weights = softmax_rows(memory_scores)
    memory_rounded = rounded(memory_weights)
    memory_result = jnp.einsum(
        "sbhqk,sbkhd->sbqhd", memory_rounded, fetched_values, preferred_element_type=jnp.float32
    )
    memory_result = memory_result.reshape(head_shape)
    attention_heads = rounded(gating[:, None] * memory_result + local_share[:, None] * local_result)
    attention_heads = attention_heads.reshape(row_total, quarter_width)
    full_weight = lax.all_gather(out_weight, "fsdp", axis=0, tiled=True)
    attention_tokens = lax.all_to_all(
        attention_heads, "fsdp", split_axis=0, concat_axis=1, tiled=True
    )
    projected = rounded(jnp.dot(attention_tokens, full_weight, preferred_element_type=jnp.float32))
    grad_tokens = rounded(
        lax.dot_general(
            cotangent, full_weight, (((1,), (1,)), ((), ())), preferred_element_type=jnp.float32
        )
    )
    attention_grad = lax.all_to_all(grad_tokens, "fsdp", split_axis=1, concat_axis=0, tiled=True)
    partial_value = lax.dot_general(
        attention_tokens, cotangent, (((0,), (0,)), ((), ())), preferred_element_type=jnp.float32
    )
    column_sums = lax.psum_scatter(
        partial_value.astype(jnp.bfloat16), "mem", scatter_dimension=1, tiled=True
    )
    weight_grad = lax.psum_scatter(column_sums, "fsdp", scatter_dimension=0, tiled=True).astype(
        jnp.float32
    )
    grad_heads = attention_grad.reshape(head_shape)
    value_grad = local_share[:, None] * jnp.einsum(
        "shqk,sqhd->skhd", local_rounded, grad_heads, preferred_element_type=jnp.float32
    )
    local_slope = local_share[None, :, None, None] * jnp.einsum(
        "sqhd,skhd->shqk", grad_heads, value_heads, preferred_element_type=jnp.float32
    )
    local_delta = rounded(
        local_weights * (local_slope - jnp.sum(local_weights * local_slope, axis=-1, keepdims=True))
    )
    block_grad = grad_heads.reshape(SEG_DEV, blocks_per_segment, QBLK, heads_here, DH)
    memory_slope = gating[None, None, :, None, None] * jnp.einsum(
        "sbqhd,sbkhd->sbhqk", block_grad, fetched_values, preferred_element_type=jnp.float32
    )
    memory_delta = rounded(
        memory_weights
        * (memory_slope - jnp.sum(memory_weights * memory_slope, axis=-1, keepdims=True))
    )
    key_grad = scaling * jnp.einsum(
        "shqk,sqhd->skhd", local_delta, query_heads, preferred_element_type=jnp.float32
    )
    memory_part = jnp.einsum(
        "sbhqk,sbkhd->sbqhd", memory_delta, fetched_keys, preferred_element_type=jnp.float32
    )
    query_grad = scaling * (
        jnp.einsum("shqk,skhd->sqhd", local_delta, key_heads, preferred_element_type=jnp.float32)
        + memory_part.reshape(head_shape)
    )
    query_out, key_out, value_out = (
        lax.all_to_all(
            rounded(query_grad).reshape(row_total, quarter_width),
            "fsdp",
            split_axis=0,
            concat_axis=1,
            tiled=True,
        ),
        lax.all_to_all(
            rounded(key_grad).reshape(row_total, quarter_width),
            "fsdp",
            split_axis=0,
            concat_axis=1,
            tiled=True,
        ),
        lax.all_to_all(
            rounded(value_grad).reshape(row_total, quarter_width),
            "fsdp",
            split_axis=0,
            concat_axis=1,
            tiled=True,
        ),
    )
    return (projected, query_out, key_out, value_out, weight_grad)


def solution(mesh):
    in_specs = (
        P(("mem", "fsdp"), None),
        P(("mem", "fsdp"), None),
        P(("mem", "fsdp"), None),
        P("mem", "fsdp"),
        P("mem", "fsdp"),
        P(),
        P(),
        P("fsdp", None),
        P(("mem", "fsdp"), None),
    )
    out_specs = (
        P(("mem", "fsdp"), None),
        P(("mem", "fsdp"), None),
        P(("mem", "fsdp"), None),
        P(("mem", "fsdp"), None),
        P("fsdp", "mem"),
    )
    return jax.shard_map(
        per_device, mesh=mesh, in_specs=in_specs, out_specs=out_specs, check_vma=False
    )
```

profile of v0, /device:TPU:0, one launch (start us, length us, event | category | flops | bytes accessed | tf_op | source)
XLA Modules:
  0.0 667.6 jit_solution(2815670768932234331)
XLA Ops:
  8.0 2.2 copy.214
  10.2 4.2 all-to-all-start.2
  15.7 2.0 copy.222
  18.1 5.2 all-to-all-done.2
  23.3 3.5 all-to-all-start.3
  26.9 6.6 gather_fusion
  33.5 8.2 %gather_fusion.2 = bf16[128,128,256]{2,1,0:T(8,128)(2,1)} fusion(bf16[32,128,256]{2,1,0:T(8,128)(2,1)} %bitcast.105, s32[1024]{0:T(1024)S(1)} %pad_clamp_fusion.1), kind=kCustom, calls=%fused_computation.2.clone | custom fusion | bytes 16777728 | tf_op jit(solution)/shard_map/jit(_take)/gather | solution.py:66
  42.8 3.5 all-to-all-start.4
  46.3 11.6 %broadcast_select_fusion = (bf16[8,2,8,128,256]{4,3,2,1,0:T(8,128)(2,1)}, bf16[8,2,8,128,256]{4,3,2,1,0:T(8,128)(2,1)}) fusion(bf16[8,2,8,128,256]{4,3,2,1,0:T(8,128)(2,1)} %bitcast.104, pred[8,2,8]{2,1,0:T(4,128)(4,1)S(1)} %compare_and_fusion, bf16[8,2,8,128,256]{4,3,2,1,0:T(8,128)(2,1)} %bitcast.103), kind=kLoop, calls=%fused_computation.25 | loop fusion | flops 8388608 | bytes 33554560 | tf_op jit(solution)/shard_map/jit(_take)/select_n | solution.py:66
  57.9 189.8 %all_to_all.150 = bf16[8,2,8,128,256]{4,3,2,1,0:T(8,128)(2,1)} all-to-all(bf16[8,2,8,128,256]{4,3,2,1,0:T(8,128)(2,1)} %get-tuple-element.32), channel_id=1, replica_groups=mesh['mem'=8,'fsdp'=4] {'mem'}, dimensions={0} | all-to-all | bytes 16777216 | tf_op jit(solution)/shard_map/all_to_all | solution.py:70
  247.6 5.2 all-to-all-start.1
  257.2 5.4 fusion.93
  262.6 28.6 %all-gather.2.cloned.1.call-done = bf16[1024,2048]{1,0:T(8,128)(2,1)} async-done(((bf16[256,2048]{1,0:T(8,128)(2,1)}), bf16[1024,2048]{1,0:T(8,128)(2,1)}) %all-gather.2.cloned.1.call-update) | async-done | bytes 4194320 | tf_op jit(solution)/shard_map/all_gather | solution.py:107
  291.2 3.5 convolution_convert_fusion.2
  295.7 6.1 gather_fusion.1
  301.8 133.8 %all-to-all-done.1 = bf16[8,2,8,128,256]{4,3,2,1,0:T(8,128)(2,1)} async-done(((bf16[8,2,8,128,256]{4,3,2,1,0:T(8,128)(2,1)}), bf16[8,2,8,128,256]{4,3,2,1,0:T(8,128)(2,1)}, u32[]{:S(2)}, u32[]{:S(2)}) %all-to-all-start.1) | async-done | bytes 8388640 | tf_op jit(solution)/shard_map/all_to_all | solution.py:69
  435.7 3.6 all-to-all-start.6
  439.3 6.2 gather_fusion.3
  445.5 5.9 broadcast_select_fusion.2
  451.4 12.9 %reshape.284 = bf16[2,4,1024,4,64]{4,3,2,1,0:T(4,128)(2,1)} reshape(bf16[64,128,256]{2,1,0:T(8,128)(2,1)} %get-tuple-element.33) | data formatting | bytes 8388608 | tf_op jit(solution)/shard_map/reshape | solution.py:79
  464.4 12.8 %copy.216 = bf16[2,4,1024,4,64]{2,4,3,1,0:T(8,128)(2,1)} copy(bf16[2,4,1024,4,64]{4,3,2,1,0:T(4,128)(2,1)} %reshape.284) | data formatting | bytes 8388608 | tf_op jit(solution)/shard_map/reshape | solution.py:79
  477.1 12.9 %reshape.283 = bf16[2,4,1024,4,64]{4,3,2,1,0:T(4,128)(2,1)} reshape(bf16[64,128,256]{2,1,0:T(8,128)(2,1)} %get-tuple-element.34) | data formatting | bytes 8388608 | tf_op jit(solution)/shard_map/reshape | solution.py:80
  490.1 12.8 %copy.218 = bf16[2,4,1024,4,64]{2,4,3,1,0:T(8,128)(2,1)} copy(bf16[2,4,1024,4,64]{4,3,2,1,0:T(4,128)(2,1)} %reshape.283) | data formatting | bytes 8388608 | tf_op jit(solution)/shard_map/reshape | solution.py:80
  502.9 10.9 %fusion.88 = (f32[2,4,4,128]{3,2,1,0:T(4,128)S(1)}, f32[2,4,4,128,1024]{3,4,2,1,0:T(8,128)}) fusion(bf16[2,4,1024,4,64]{2,4,3,1,0:T(8,128)(2,1)} %copy.216, bf16[2,4,128,4,64]{2,1,0,4,3:T(4,128)(2,1)S(1)} %copy-done.8), kind=kOutput, calls=%fused_computation.103 | convolution fusion | flops 549454848 | bytes 21512192 | tf_op jit(solution)/shard_map/sub | solution.py:17
  513.8 8.5 %fusion.35 = f32[2,4,4,8,8,128]{5,4,3,2,1,0:T(8,128)S(1)} fusion(bf16[2,4,1024,4,64]{2,4,3,1,0:T(8,128)(2,1)} %copy.218, f32[2,4,4,128,1024]{3,4,2,1,0:T(8,128)} %get-tuple-element.36, f32[2,4,4,128]{3,2,1,0:T(4,128)S(1)} %get-tuple-element.35), kind=kOutput, calls=%fused_computation.44 | convolution fusion | flops 545259520 | bytes 22036480 | tf_op jit(solution)/shard_map/sbhqk,sbkhd->sbqhd/dot_general | solution.py:101
  522.3 4.4 fusion.42
  528.3 3.6 all-to-all-start.5
  533.9 6.8 %all-to-all-done.5 = bf16[4,256,256]{1,2,0:T(8,128)(2,1)S(1)} async-done(((bf16[4,256,256]{1,2,0:T(8,128)(2,1)}), bf16[4,256,256]{1,2,0:T(8,128)(2,1)S(1)}, u32[]{:S(2)}, u32[]{:S(2)}) %all-to-all-start.5) | async-done | bytes 524320 | tf_op jit(solution)/shard_map/all_to_all | solution.py:108
  540.7 4.4 convolution_convert_fusion
  545.2 4.6 multiply_reduce_fusion.1
  549.8 5.0 multiply_convert_fusion.2
  554.8 1.9 copy-done.2
  556.7 1.4 fusion.49
  559.8 3.5 all-to-all-start.8
  563.2 4.9 fusion.50
  569.8 12.7 %multiply_reduce_fusion = (f32[2,4,4,128]{3,2,1,0:T(4,128)S(1)}, f32[2,4,4,128,1024]{3,4,2,1,0:T(8,128)}) fusion(f32[4]{0:T(128)S(1)} %get-tuple-element.28, f32[2,4,4,128,1024]{3,4,2,1,0:T(8,128)} %get-tuple-element.36, f32[2,4,4,128]{3,2,1,0:T(4,128)S(1)} %get-tuple-element.35, bf16[2,4,1024,4,64]{2,4,3,1,0:T(8,128)(2,1)} %copy.218, ...), kind=kOutput, calls=%fused_computation.11 | convolution fusion | flops 553644032 | bytes 38305808 | tf_op jit(solution)/shard_map/sbqhd,sbkhd->sbhqk/dot_general | solution.py:138
  582.5 4.2 all-to-all-start.9
  587.0 16.2 %fusion.40 = f32[2,4,4,8,8,128]{5,4,3,2,1,0:T(8,128)} fusion(bf16[2,4,1024,4,64]{2,4,3,1,0:T(8,128)(2,1)} %copy.216, f32[2,4,4,128,1024]{3,4,2,1,0:T(8,128)} %get-tuple-element.42, f32[2,4,4,128]{3,2,1,0:T(4,128)S(1)} %get-tuple-element.41, f32[4]{0:T(128)S(1)} %get-tuple-element.28, f32[2,4,4,128,1024]{3,4,2,1,0:T(8,128)} %get-tuple-element.36, ...), kind=kOutput, calls=%fused_computation.49 | convolution fusion | flops 557842432 | bytes 38830096 | tf_op jit(solution)/shard_map/sbhqk,sbkhd->sbqhd/dot_general | solution.py:148
  603.2 28.5 %reduce-scatter.3.cloned.1.call-done = bf16[1024,256]{1,0:T(8,128)(2,1)} async-done(((bf16[1024,2048]{1,0:T(8,128)(2,1)}), bf16[1024,256]{1,0:T(8,128)(2,1)}) %reduce-scatter.3.cloned.1.call-update) | async-done | bytes 524304 | tf_op jit(solution)/shard_map/reduce_scatter | solution.py:121
  631.7 3.4 fusion.41
  636.7 1.9 copy.246
  638.6 3.5 all-to-all-start.7
  642.1 2.0 copy.256
  644.1 2.0 copy.257
  646.1 6.5 all-to-all-done.7
  652.7 1.0 copy.255
  653.7 4.5 convolution_convert_fusion.1
  658.1 1.6 convert_element_type.59
  (73 shorter events, 16.7 us)
Async XLA Ops:
  8.0 18.9 %copy-start = (bf16[4096,256]{1,0:T(8,128)(2,1)S(1)}, bf16[4096,256]{1,0:T(8,128)(2,1)}, u32[]{:S(2)}) copy-start(bf16[4096,256]{1,0:T(8,128)(2,1)} %param.17) | copy-start | bytes 6291460
  10.2 13.1 %all-to-all-start.2 = ((bf16[256,4,256]{0,2,1:T(8,128)(2,1)}), bf16[256,4,256]{0,2,1:T(8,128)(2,1)S(1)}, u32[]{:S(2)}, u32[]{:S(2)}) async-start(bf16[256,4,256]{0,2,1:T(8,128)(2,1)} %bitcast.8), calls=%async_computation.2 | async-start | bytes 1048576 | tf_op jit(solution)/shard_map/all_to_all | solution.py:42
  23.3 19.5 %all-to-all-start.3 = ((bf16[256,4,256]{0,2,1:T(8,128)(2,1)}), bf16[256,4,256]{0,2,1:T(8,128)(2,1)S(1)}, u32[]{:S(2)}, u32[]{:S(2)}) async-start(bf16[256,4,256]{0,2,1:T(8,128)(2,1)} %bitcast.114), calls=%async_computation.3 | async-start | bytes 1048576 | tf_op jit(solution)/shard_map/all_to_all | solution.py:43
  33.5 8.2 %copy-start.5 = (bf16[256,1024]{1,0:T(8,128)(2,1)S(1)}, bf16[256,1024]{1,0:T(8,128)(2,1)}, u32[]{:S(2)}) copy-start(bf16[256,1024]{1,0:T(8,128)(2,1)} %param.15) | copy-start | bytes 1572868
  42.8 15.1 %all-to-all-start.4 = ((bf16[256,4,256]{0,2,1:T(8,128)(2,1)}), bf16[256,4,256]{0,2,1:T(8,128)(2,1)S(1)}, u32[]{:S(2)}, u32[]{:S(2)}) async-start(bf16[256,4,256]{0,2,1:T(8,128)(2,1)} %bitcast.14), calls=%async_computation.4 | async-start | bytes 1048576 | tf_op jit(solution)/shard_map/all_to_all | solution.py:44
  247.6 6.0 copy-start.10
  247.6 188.0 %all-to-all-start.1 = ((bf16[8,2,8,128,256]{4,3,2,1,0:T(8,128)(2,1)}), bf16[8,2,8,128,256]{4,3,2,1,0:T(8,128)(2,1)}, u32[]{:S(2)}, u32[]{:S(2)}) async-start(bf16[8,2,8,128,256]{4,3,2,1,0:T(8,128)(2,1)} %get-tuple-element.31), calls=%async_computation.1 | async-start | bytes 16777216 | tf_op jit(solution)/shard_map/all_to_all | solution.py:69
  252.8 38.4 %all-gather.2.cloned.1.call-start = ((), (), s32[]{:S(2)}) async-start(), calls=%async_computation.12 | async-start | bytes 5242880 | tf_op jit(solution)/shard_map/all_gather | solution.py:107
  256.8 34.4 %copy-start.4 = (bf16[256,2048]{1,0:T(8,128)(2,1)S(1)}, bf16[256,2048]{1,0:T(8,128)(2,1)}, u32[]{:S(2)}) copy-start(bf16[256,2048]{1,0:T(8,128)(2,1)} %param.21) | copy-start | bytes 3145732
  257.1 265.2 %copy-start.6 = (bf16[2,512,4,64]{1,0,3,2:T(2,128)(2,1)}, bf16[2,512,4,64]{1,0,3,2:T(2,128)(2,1)S(1)}, u32[]{:S(2)}) copy-start(bf16[2,512,4,64]{1,0,3,2:T(2,128)(2,1)S(1)} %reshape.230) | copy-start | bytes 1572868
  435.7 92.6 %all-to-all-start.6 = ((bf16[256,4,256]{0,2,1:T(8,128)(2,1)}), bf16[256,4,256]{0,2,1:T(8,128)(2,1)S(1)}, u32[]{:S(2)}, u32[]{:S(2)}) async-start(bf16[256,4,256]{0,2,1:T(8,128)(2,1)} %bitcast.19), calls=%async_computation.6 | async-start | bytes 1048576 | tf_op jit(solution)/shard_map/all_to_all | solution.py:117
  490.1 12.8 %copy-start.8 = (bf16[2,4,128,4,64]{2,1,0,4,3:T(4,128)(2,1)S(1)}, bf16[2,4,128,4,64]{2,1,0,4,3:T(4,128)(2,1)}, u32[]{:S(2)}) copy-start(bf16[2,4,128,4,64]{2,1,0,4,3:T(4,128)(2,1)} %reshape_reshape.6) | copy-start | bytes 1572868
  528.3 16.9 %copy-start.7 = (bf16[2,512,4,64]{1,0,3,2:T(2,128)(2,1)S(1)}, bf16[2,512,4,64]{1,0,3,2:T(2,128)(2,1)}, u32[]{:S(2)}) copy-start(bf16[2,512,4,64]{1,0,3,2:T(2,128)(2,1)} %copy-done.6) | copy-start | bytes 1572868
  528.3 12.4 %all-to-all-start.5 = ((bf16[4,256,256]{1,2,0:T(8,128)(2,1)}), bf16[4,256,256]{1,2,0:T(8,128)(2,1)S(1)}, u32[]{:S(2)}, u32[]{:S(2)}) async-start(bf16[4,256,256]{1,2,0:T(8,128)(2,1)} %copy.231), calls=%async_computation.5 | async-start | bytes 1048576 | tf_op jit(solution)/shard_map/all_to_all | solution.py:108
  531.9 99.7 %reduce-scatter.3.cloned.1.call-start = ((), (), s32[]{:S(2)}) async-start(), calls=%async_computation.13 | async-start | bytes 4718592 | tf_op jit(solution)/shard_map/reduce_scatter | solution.py:121
  554.8 1.9 copy-start.2
  559.8 22.8 %all-to-all-start.8 = ((bf16[4,256,256]{1,2,0:T(8,128)(2,1)}), bf16[4,256,256]{1,2,0:T(8,128)(2,1)S(1)}, u32[]{:S(2)}, u32[]{:S(2)}) async-start(bf16[4,256,256]{1,2,0:T(8,128)(2,1)} %copy.250), calls=%async_computation.8 | async-start | bytes 1048576 | tf_op jit(solution)/shard_map/all_to_all | solution.py:163
  563.2 6.6 copy-start.9
  582.5 20.6 %copy-start.3 = (bf16[4,256,256]{1,2,0:T(8,128)(2,1)}, bf16[4,256,256]{1,2,0:T(8,128)(2,1)S(1)}, u32[]{:S(2)}) copy-start(bf16[4,256,256]{1,2,0:T(8,128)(2,1)S(1)} %all-to-all-done.8) | copy-start | bytes 1572868
  582.5 56.0 %all-to-all-start.9 = ((bf16[4,256,256]{1,2,0:T(8,128)(2,1)}), bf16[4,256,256]{1,2,0:T(8,128)(2,1)}, u32[]{:S(2)}, u32[]{:S(2)}) async-start(bf16[4,256,256]{1,2,0:T(8,128)(2,1)} %copy.254), calls=%async_computation.9 | async-start | bytes 1048576 | tf_op jit(solution)/shard_map/all_to_all | solution.py:170
  586.7 71.4 %reduce-scatter.5.cloned.1.call-start = ((), (), s32[]{:S(2)}) async-start(), calls=%async_computation.14 | async-start | bytes 655360 | tf_op jit(solution)/shard_map/reduce_scatter | solution.py:124
  631.7 28.1 %copy-start.1 = (bf16[4096,256]{1,0:T(8,128)(2,1)S(1)}, bf16[4096,256]{1,0:T(8,128)(2,1)}, u32[]{:S(2)}) copy-start(bf16[4096,256]{1,0:T(8,128)(2,1)} %param.17) | copy-start | bytes 6291460
  638.6 14.1 %all-to-all-start.7 = ((bf16[4,256,256]{1,2,0:T(8,128)(2,1)}), bf16[4,256,256]{1,2,0:T(8,128)(2,1)S(1)}, u32[]{:S(2)}, u32[]{:S(2)}) async-start(bf16[4,256,256]{1,2,0:T(8,128)(2,1)} %copy.246), calls=%async_computation.7 | async-start | bytes 1048576 | tf_op jit(solution)/shard_map/all_to_all | solution.py:156
Sparse Core Ops, SparseCore 0:
  255.2 35.9 all-gather.1
  631.8 22.7 reduce-scatter.4
Sparse Core Ops, SparseCore 1:
  545.3 86.3 reduce-scatter.2
where the time goes:
time: 679 us; the launch traced here: 668 us
  waiting for transfers between devices  210 us (31%)
  blocking collectives  190 us (28%)
  local copies, waits for them, and re-layouts  106 us (16%)
  matrix products  84.8 us (12%)
  starting transfers between devices  35.3 us (5%)
  other arithmetic  25.2 us (4%)
  between operations  16.3 us (2%)
    all_to_all x1, blocking collectives, per_device(): lax.all_to_all(send_values, 'mem', split_axis=0, concat_axis=0, tiled=True)  190 us
    all_to_all x1, waiting for transfers between devices, per_device(): lax.all_to_all(send_keys, 'mem', split_axis=0, concat_axis=0, tiled=True)  134 us
    all_gather x1, waiting for transfers between devices, per_device(): full_weight = lax.all_gather(out_weight, 'fsdp', axis=0, tiled=True)  28.6 us
    reduce_scatter x1, waiting for transfers between devices, per_device(): lax.psum_scatter(partial_value.astype(jnp.bfloat16), 'mem', scatter_dimen...  28.5 us
    reshape x2, local copies, waits for them, and re-layouts, per_device(): jnp.take(flat_values, slot_index, axis=0).reshape(block_shape)  25.7 us
    reshape x2, local copies, waits for them, and re-layouts, per_device(): fetched_keys = jnp.take(flat_keys, slot_index, axis=0).reshape(block_shape)  25.7 us
    sub x2, matrix products, softmax_rows(): weights = jnp.exp(scores - largest)  16.3 us
    dot_general x1, matrix products, per_device(): jnp.einsum('sbhqk,sbkhd->sbqhd', memory_delta, fetched_keys, preferred_el...  16.2 us
  transfers between devices with their start and end apart: 12, of which 6 were waited for; matrix products, arithmetic and copies ran while one was open for 31% of the time, Pallas kernels for 0%

commit v1 on v0

v1 whole, which is shorter than its diff:
```python
import functools

import jax
import jax.numpy as jnp
from jax import lax
from jax.experimental import pallas as pl
from jax.experimental.pallas import tpu as pltpu
from jax.sharding import PartitionSpec as P

DH = 64
QBLK = 128
MBLK = 128
LOW = -1e30
SCALE = DH ** (-0.5)
BF = jnp.bfloat16
F32 = jnp.float32
NT = (((1,), (1,)), ((), ()))
NN = (((1,), (0,)), ((), ()))
TN = (((0,), (0,)), ((), ()))


def dot(a, b, dims):
    return lax.dot_general(a, b, dims, preferred_element_type=F32)


def spread(x):
    lane = lax.broadcasted_iota(jnp.int32, x.shape, 1)
    zero = jnp.zeros_like(x)
    return jnp.concatenate(
        [jnp.where(lane < DH, x, zero), jnp.where(lane >= DH, x, zero)], axis=0
    )


def folded(x, op):
    return op(x.reshape(x.shape[0] // 8, 8, x.shape[1]), axis=0)


def own_blocks(parts):
    rows = []
    for part in parts:
        rows.append(part[:DH, :QBLK])
        rows.append(part[DH:, QBLK:])
    return rows


def load_memory(sources, targets, sems):
    copies = []
    for number, (source, target) in enumerate(zip(sources, targets)):
        copy = pltpu.make_async_copy(source, target, sems.at[number])
        copy.start()
        copies.append(copy)
    for copy in copies:
        copy.wait()


def at_slot(slot, total, per_slot, lead=0):
    def index(s, b, *_):
        block = jnp.where(s == slot, b, jnp.where(s > slot, per_slot - 1, 0))
        return (block,) + (0,) * lead

    return index


def memory_forward(
    group, pairs, counts, lists, k_own, v_own, k_par, v_par, *rest
):
    q_refs = rest[:group]
    do_refs = rest[group : 2 * group]
    o_refs = rest[2 * group : 3 * group]
    stat_ref = rest[3 * group]
    kbuf, vbuf, qbd, dobd, scores, slopes, acc, sems = rest[3 * group + 1 :]
    slot, block = pl.program_id(0), pl.program_id(1)
    number = slot * pl.num_programs(1) + block
    rows = k_own.shape[0]
    retr = scores.shape[0]

    @pl.when(number == 0)
    def _():
        load_memory(
            (k_own, k_par, v_own, v_par),
            (
                kbuf.at[pl.ds(0, rows)],
                kbuf.at[pl.ds(rows, rows)],
                vbuf.at[pl.ds(0, rows)],
                vbuf.at[pl.ds(rows, rows)],
            ),
            sems,
        )

    for i in range(group):

        @pl.when(slot == i)
        def _():
            for t in range(pairs):
                cols = slice(t * 128, (t + 1) * 128)
                qbd[t] = spread(q_refs[i][:, cols] * SCALE)
                dobd[t] = spread(do_refs[i][:, cols])

    total = counts[number]

    def first(j, largest):
        row = pl.multiple_of(lists[number * retr + j] * MBLK, MBLK)
        out = []
        for t in range(pairs):
            cols = slice(t * 128, (t + 1) * 128)
            wide = slice(t * 256, (t + 1) * 256)
            s = dot(kbuf[pl.ds(row, MBLK), cols], qbd[t], NT)
            scores[j, :, wide] = s
            slopes[j, :, wide] = dot(vbuf[pl.ds(row, MBLK), cols], dobd[t], NT)
            out.append(jnp.maximum(largest[t], folded(s, jnp.max)))
        return tuple(out)

    largest = lax.fori_loop(0, total, first, (jnp.full((8, 256), LOW, F32),) * pairs)
    largest = [jnp.max(x, axis=0, keepdims=True) for x in largest]
    acc[...] = jnp.zeros_like(acc)

    def second(j, sums):
        row = pl.multiple_of(lists[number * retr + j] * MBLK, MBLK)
        out = []
        for t in range(pairs):
            cols = slice(t * 128, (t + 1) * 128)
            wide = slice(t * 256, (t + 1) * 256)
            p = jnp.exp(scores[j, :, wide] - largest[t])
            acc[t] += dot(vbuf[pl.ds(row, MBLK), cols], p.astype(BF), TN)
            out.append(
                (
                    sums[t][0] + folded(p, jnp.sum),
                    sums[t][1] + folded(p * slopes[j, :, wide], jnp.sum),
                )
            )
        return tuple(out)

    zero = jnp.zeros((8, 256), F32)
    sums = lax.fori_loop(0, total, second, ((zero, zero),) * pairs)
    parts = []
    for t in range(pairs):
        wide = slice(t * 256, (t + 1) * 256)
        norm = jnp.sum(sums[t][0], axis=0, keepdims=True)
        mean = jnp.sum(sums[t][1], axis=0, keepdims=True)
        some = norm > 0.0
        inverse = jnp.where(some, 1.0 / jnp.where(some, norm, 1.0), 0.0)
        lse = jnp.where(some, largest[t] + jnp.log(jnp.where(some, norm, 1.0)), LOW)
        stat_ref[0, 0, 0:1, wide] = lse
        stat_ref[0, 0, 1:2, wide] = mean * inverse
        parts.append(acc[t] * inverse)
    result = jnp.concatenate(own_blocks(parts), axis=0).astype(BF)
    for i in range(group):

        @pl.when(slot == i)
        def _():
            o_refs[i][0] = result


def merged(stat_refs):
    lses = [ref[0, 0, 0:1, :] for ref in stat_refs]
    top = functools.reduce(jnp.maximum, lses)
    shares = [jnp.exp(x - top) for x in lses]
    norm = functools.reduce(jnp.add, shares)
    return top, shares, norm


def memory_backward(
    group, pairs, counts, lists, k_own, v_own, k_par, v_par, *rest
):
    q_refs = rest[:group]
    do_refs = rest[group : 2 * group]
    stat_refs = rest[2 * group : 3 * group]
    dq_refs = rest[3 * group : 4 * group]
    kbuf, vbuf, qbd, dobd, acc, sems = rest[4 * group :]
    slot, block = pl.program_id(0), pl.program_id(1)
    number = slot * pl.num_programs(1) + block
    rows = k_own.shape[0]
    retr = lists.shape[0] // counts.shape[0]

    @pl.when(number == 0)
    def _():
        load_memory(
            (k_own, k_par, v_own, v_par),
            (
                kbuf.at[pl.ds(0, rows)],
                kbuf.at[pl.ds(rows, rows)],
                vbuf.at[pl.ds(0, rows)],
                vbuf.at[pl.ds(rows, rows)],
            ),
            sems,
        )

    for i in range(group):

        @pl.when(slot == i)
        def _():
            for t in range(pairs):
                cols = slice(t * 128, (t + 1) * 128)
                qbd[t] = spread(q_refs[i][:, cols] * SCALE)
                dobd[t] = spread(do_refs[i][:, cols])

    top, shares, norm = merged(stat_refs)
    lse = top + jnp.log(norm)
    mean = functools.reduce(
        jnp.add, [x * ref[0, 0, 1:2, :] for x, ref in zip(shares, stat_refs)]
    ) / norm
    acc[...] = jnp.zeros_like(acc)

    def step(j, carry):
        row = pl.multiple_of(lists[number * retr + j] * MBLK, MBLK)
        for t in range(pairs):
            cols = slice(t * 128, (t + 1) * 128)
            wide = slice(t * 256, (t + 1) * 256)
            keys = kbuf[pl.ds(row, MBLK), cols]
            s = dot(keys, qbd[t], NT)
            slope = dot(vbuf[pl.ds(row, MBLK), cols], dobd[t], NT)
            delta = jnp.exp(s - lse[:, wide]) * (slope - mean[:, wide])
            acc[t] += dot(keys, delta.astype(BF), TN)
        return carry

    lax.fori_loop(0, counts[number], step, 0)
    result = jnp.concatenate(own_blocks([acc[t] for t in range(pairs)]), axis=0).astype(BF)
    for i in range(group):

        @pl.when(slot == i)
        def _():
            dq_refs[i][0] = result


def local_kernel(pairs, blocks, gate, q_ref, k_ref, v_ref, do_ref, o_ref, dq_ref, dk_ref, dv_ref,
                 dk_acc, dv_acc):
    dk_acc[...] = jnp.zeros_like(dk_acc)
    dv_acc[...] = jnp.zeros_like(dv_acc)
    key_at = lax.broadcasted_iota(jnp.int32, (MBLK, 2 * QBLK), 0)
    query_at = lax.broadcasted_iota(jnp.int32, (MBLK, 2 * QBLK), 1) % QBLK
    causal = key_at <= query_at
    lane = lax.broadcasted_iota(jnp.int32, (1, 128), 1)
    shares = []
    for t in range(pairs):
        shares.append(jnp.where(lane < DH, 1.0 - gate[2 * t], 1.0 - gate[2 * t + 1]))
    for t in range(pairs):
        cols = slice(t * 128, (t + 1) * 128)
        for b in range(blocks):
            q = spread(q_ref[b * QBLK : (b + 1) * QBLK, cols] * SCALE)
            do = spread(do_ref[b * QBLK : (b + 1) * QBLK, cols])
            scores, slopes = [], []
            for n in range(b + 1):
                rows = slice(n * MBLK, (n + 1) * MBLK)
                s = dot(k_ref[rows, cols], q, NT)
                scores.append(jnp.where(causal, s, LOW) if n == b else s)
                slopes.append(dot(v_ref[rows, cols], do, NT))
            largest = functools.reduce(jnp.maximum, [folded(s, jnp.max) for s in scores])
            largest = jnp.max(largest, axis=0, keepdims=True)
            weights = [jnp.exp(s - largest) for s in scores]
            norm = functools.reduce(jnp.add, [folded(p, jnp.sum) for p in weights])
            inverse = 1.0 / jnp.sum(norm, axis=0, keepdims=True)
            weights = [p * inverse for p in weights]
            mean = functools.reduce(
                jnp.add, [folded(p * x, jnp.sum) for p, x in zip(weights, slopes)]
            )
            mean = jnp.sum(mean, axis=0, keepdims=True)
            o = jnp.zeros((128, 256), F32)
            dq = jnp.zeros((128, 256), F32)
            for n in range(b + 1):
                rows = slice(n * MBLK, (n + 1) * MBLK)
                w = weights[n].astype(BF)
                delta = (weights[n] * (slopes[n] - mean)).astype(BF)
                o += dot(v_ref[rows, cols], w, TN)
                dq += dot(k_ref[rows, cols], delta, TN)
                dv_acc[rows, cols] += dot(w, do, NN)
                dk_acc[rows, cols] += dot(delta, q, NN)
            o_pair, dq_pair = own_blocks([o]), own_blocks([dq])
            for i in range(2):
                share = 1.0 - gate[2 * t + i]
                at = slice((2 * t + i) * DH, (2 * t + i + 1) * DH)
                o_ref[b, at, :] = o_pair[i] * share
                dq_ref[b, at, :] = dq_pair[i] * (share * SCALE)
        dk_ref[:, cols] = (dk_acc[:, cols] * shares[t]).astype(BF)
        dv_ref[:, cols] = (dv_acc[:, cols] * shares[t]).astype(BF)


def attention_kernel(group, heads, gate, local_ref, *rest):
    o_refs = rest[:group]
    stat_refs = rest[group : 2 * group]
    out_ref = rest[2 * group]
    _, shares, norm = merged(stat_refs)
    rows = []
    for h in range(heads):
        at = slice(h * DH, (h + 1) * DH)
        wide = slice(h * QBLK, (h + 1) * QBLK)
        total = functools.reduce(
            jnp.add,
            [x[:, wide] * ref[0, at, :].astype(F32) for x, ref in zip(shares, o_refs)],
        )
        rows.append(total * (gate[h] / norm[:, wide]) + local_ref[0, at, :])
    out_ref[...] = jnp.concatenate(rows, axis=0).T.astype(BF)


def query_grad_kernel(group, heads, gate, local_ref, *rest):
    dq_refs = rest[:group]
    out_ref = rest[group]
    rows = []
    for h in range(heads):
        at = slice(h * DH, (h + 1) * DH)
        total = functools.reduce(jnp.add, [ref[0, at, :].astype(F32) for ref in dq_refs])
        rows.append(total * (gate[h] * SCALE) + local_ref[0, at, :])
    out_ref[...] = jnp.concatenate(rows, axis=0).T.astype(BF)


ANY = pl.BlockSpec(memory_space=pl.ANY)
SMEM = pl.BlockSpec(memory_space=pltpu.SMEM)


def block_lists(block_ids, me, group, seg_dev, per_dev):
    segments, per_seg, retr = block_ids.shape
    z = me // 2
    ids = block_ids.reshape(segments // (2 * seg_dev), 2, seg_dev * per_seg, retr)
    ids = lax.dynamic_index_in_dim(ids, me % 2, 1, keepdims=False)
    slots = (z - jnp.arange(group, dtype=jnp.int32)) % group
    ids = jnp.take(ids, slots, axis=0).reshape(group * seg_dev * per_seg, retr)
    owners = ids // per_dev
    here = owners // 2 == z
    place = ids - owners * per_dev + jnp.where(owners == me, 0, per_dev)
    position = jnp.arange(retr, dtype=jnp.int32)
    before = (position[None, :] < position[:, None])[None]
    rank = jnp.sum(jnp.logical_and(before, here[:, None, :]), axis=-1)
    chosen = jnp.logical_and(here[:, :, None], rank[:, :, None] == position)
    lists = jnp.sum(jnp.where(chosen, place[:, :, None], 0), axis=1)
    counts = jnp.sum(here, axis=-1)
    return counts.astype(jnp.int32), lists.astype(jnp.int32).reshape(-1)


def to_heads(x):
    parts = lax.axis_size("fsdp")
    rows, width = x.shape
    x = x.reshape(rows, parts, width // parts).transpose(1, 0, 2)
    x = lax.all_to_all(x, "fsdp", split_axis=0, concat_axis=0, tiled=True)
    return x.reshape(parts * rows, width // parts)


def to_tokens(x):
    parts = lax.axis_size("fsdp")
    x = x.reshape(parts, x.shape[0] // parts, x.shape[1])
    return lax.all_to_all(x, "fsdp", split_axis=0, concat_axis=0, tiled=True)


def side_by_side(x):
    parts, rows, width = x.shape
    return x.transpose(1, 0, 2).reshape(rows, parts * width)


def gather_tokens(x):
    parts = lax.axis_size("fsdp")
    if parts != 4:
        return lax.all_gather(x, "fsdp", axis=0, tiled=True)
    f = lax.axis_index("fsdp")
    rows = x.shape[0]
    far = lax.ppermute(x, "fsdp", [(i, i ^ 2) for i in range(4)])
    near = lax.ppermute(x, "fsdp", [(i, i ^ 1) for i in range(4)])
    both = lax.ppermute(far, "fsdp", [(i, i ^ 1) for i in range(4)])
    out = jnp.zeros((4 * rows, x.shape[1]), x.dtype)
    for part, at in ((x, f), (near, f ^ 1), (far, f ^ 2), (both, f ^ 3)):
        out = lax.dynamic_update_slice_in_dim(out, part, at * rows, 0)
    return out


def per_device(
    queries, keys, values, mem_keys, mem_values, block_ids, gate_bias, out_weight, cotangent
):
    n = lax.axis_size("mem")
    me = lax.axis_index("mem")
    group = n // 2
    width = mem_keys.shape[1]
    heads = width // DH
    pairs = heads // 2
    segments, per_seg, retr = block_ids.shape
    seg_dev = segments // n
    per_dev = mem_keys.shape[0] // MBLK
    blocks = seg_dev * per_seg
    tokens = blocks * QBLK
    seg_len = per_seg * QBLK
    gating = jax.nn.sigmoid(
        lax.dynamic_slice_in_dim(gate_bias, lax.axis_index("fsdp") * heads, heads)
    )

    def shifted(x, k):
        return lax.ppermute(x, "mem", [(i, (i + 2 * k) % n) for i in range(n)])

    swap = [(i, i ^ 1) for i in range(n)]
    par_keys = lax.ppermute(mem_keys, "mem", swap)
    par_values = lax.ppermute(mem_values, "mem", swap)

    q = to_heads(queries)
    q_slots = [q] + [shifted(q, k) for k in range(1, group)]
    cot = gather_tokens(cotangent)
    do = dot(cot, out_weight, NT).astype(BF)
    do_slots = [do] + [shifted(do, k) for k in range(1, group)]
    k = to_heads(keys)
    v = to_heads(values)
    full_weight = lax.all_gather(out_weight, "fsdp", axis=0, tiled=True)
    counts, lists = block_lists(block_ids, me, group, seg_dev, per_dev)

    seg_spec = pl.BlockSpec((seg_len, width), lambda s: (s, 0))
    part_spec = pl.BlockSpec((per_seg, width, QBLK), lambda s: (s, 0, 0))
    part_shape = jax.ShapeDtypeStruct((blocks, width, QBLK), F32)
    head_shape = jax.ShapeDtypeStruct((tokens, width), BF)
    o_local, dq_local, dk, dv = pl.pallas_call(
        functools.partial(local_kernel, pairs, per_seg),
        grid=(seg_dev,),
        in_specs=[SMEM, seg_spec, seg_spec, seg_spec, seg_spec],
        out_specs=[part_spec, part_spec, seg_spec, seg_spec],
        out_shape=[part_shape, part_shape, head_shape, head_shape],
        scratch_shapes=[pltpu.VMEM((seg_len, width), F32), pltpu.VMEM((seg_len, width), F32)],
        compiler_params=pltpu.CompilerParams(vmem_limit_bytes=32 * 2**20),
        name="local",
    )(gating, q, k, v, do)

    row_specs = [
        pl.BlockSpec((QBLK, width), at_slot(i, group, blocks, 1)) for i in range(group)
    ]
    t_specs = [
        pl.BlockSpec((1, width, QBLK), at_slot(i, group, blocks, 2)) for i in range(group)
    ]
    t_shape = jax.ShapeDtypeStruct((blocks, width, QBLK), BF)
    stat_block = (1, 1, 2, heads * QBLK)
    memory_rows = 2 * mem_keys.shape[0]
    buffers = [pltpu.VMEM((memory_rows, width), BF), pltpu.VMEM((memory_rows, width), BF)]
    spreads = [pltpu.VMEM((pairs, 256, 128), BF), pltpu.VMEM((pairs, 256, 128), BF)]
    acc = pltpu.VMEM((pairs, 128, 256), F32)
    limit = pltpu.CompilerParams(vmem_limit_bytes=40 * 2**20)
    memory = (mem_keys, mem_values, par_keys, par_values)
    outs = pl.pallas_call(
        functools.partial(memory_forward, group, pairs),
        grid_spec=pltpu.PrefetchScalarGridSpec(
            num_scalar_prefetch=2,
            grid=(group, blocks),
            in_specs=[ANY] * 4 + row_specs * 2,
            out_specs=t_specs + [pl.BlockSpec(stat_block, lambda s, b, *_: (s, b, 0, 0))],
            scratch_shapes=buffers
            + spreads
            + [pltpu.VMEM((retr, MBLK, heads * QBLK), F32)] * 2
            + [acc, pltpu.SemaphoreType.DMA((4,))],
        ),
        out_shape=[t_shape] * group
        + [jax.ShapeDtypeStruct((group, blocks, 2, heads * QBLK), F32)],
        compiler_params=limit,
        name="memory_forward",
    )(counts, lists, *memory, *q_slots, *do_slots)
    o_slots, stats = outs[:group], outs[group]
    stat_slots = [stats] + [shifted(stats, k) for k in range(1, group)]
    o_home = [o_slots[0]] + [shifted(o_slots[k], -k) for k in range(1, group)]

    stat_specs = [
        pl.BlockSpec(stat_block, lambda s, b, *_, k=k: ((s - k) % group, b, 0, 0))
        for k in range(group)
    ]
    dq_slots = pl.pallas_call(
        functools.partial(memory_backward, group, pairs),
        grid_spec=pltpu.PrefetchScalarGridSpec(
            num_scalar_prefetch=2,
            grid=(group, blocks),
            in_specs=[ANY] * 4 + row_specs * 2 + stat_specs,
            out_specs=t_specs,
            scratch_shapes=buffers + spreads + [acc, pltpu.SemaphoreType.DMA((4,))],
        ),
        out_shape=[t_shape] * group,
        compiler_params=limit,
        name="memory_backward",
    )(counts, lists, *memory, *q_slots, *do_slots, *stat_slots)
    dq_home = [dq_slots[0]] + [shifted(dq_slots[k], -k) for k in range(1, group)]

    home_spec = pl.BlockSpec((1, width, QBLK), lambda b: (b, 0, 0))
    home_out = pl.BlockSpec((QBLK, width), lambda b: (b, 0))
    home_stats = [stat_slots[(group - k) % group] for k in range(group)]
    home_specs = [
        pl.BlockSpec(stat_block, lambda b, k=k: (k, b, 0, 0)) for k in range(group)
    ]
    attention = pl.pallas_call(
        functools.partial(attention_kernel, group, heads),
        grid=(blocks,),
        in_specs=[SMEM] + [home_spec] * (1 + group) + home_specs,
        out_specs=home_out,
        out_shape=head_shape,
        name="attention",
    )(gating, o_local, *o_home, *home_stats)
    dq = pl.pallas_call(
        functools.partial(query_grad_kernel, group, heads),
        grid=(blocks,),
        in_specs=[SMEM] + [home_spec] * (1 + group),
        out_specs=home_out,
        out_shape=head_shape,
        name="query_grad",
    )(gating, dq_local, *dq_home)

    token_attention = to_tokens(attention)
    parts = token_attention.shape[0]
    projected = jnp.einsum(
        "stc,scd->td",
        token_attention,
        full_weight.reshape(parts, width, -1),
        preferred_element_type=F32,
    ).astype(BF)
    partial = dot(attention, cot, TN).astype(BF)
    columns = partial.shape[1] // n
    partial = partial.reshape(width, n, columns).transpose(1, 0, 2)
    partial = lax.all_to_all(partial, "mem", split_axis=0, concat_axis=0, tiled=True)
    weight_grad = jnp.sum(partial.astype(F32), axis=0)
    return (
        projected,
        side_by_side(to_tokens(dq)),
        side_by_side(to_tokens(dk)),
        side_by_side(to_tokens(dv)),
        weight_grad,
    )


def solution(mesh):
    in_specs = (
        P(("mem", "fsdp"), None),
        P(("mem", "fsdp"), None),
        P(("mem", "fsdp"), None),
        P("mem", "fsdp"),
        P("mem", "fsdp"),
        P(),
        P(),
        P("fsdp", None),
        P(("mem", "fsdp"), None),
    )
    out_specs = (
        P(("mem", "fsdp"), None),
        P(("mem", "fsdp"), None),
        P(("mem", "fsdp"), None),
        P(("mem", "fsdp"), None),
        P("fsdp", "mem"),
    )
    return jax.shard_map(
        per_device, mesh=mesh, in_specs=in_specs, out_specs=out_specs, check_vma=False
    )
```

time: 679 us -> 467 us (0.69); the launches traced: 668 us -> 463 us
  blocking collectives: 190 us -> 44.1 us
  Pallas kernels: 0 us -> 111 us
  matrix products: 84.8 us -> 12 us
  local copies, waits for them, and re-layouts: 106 us -> 39 us
  waiting for transfers between devices: 210 us -> 150 us
  starting transfers between devices: 35.3 us -> 91.4 us
  other arithmetic: 25.2 us -> 1.33 us
    all_to_all x1, blocking collectives: 190 us -> 44.1 us  [per_device(): lax.all_to_all(partial, 'mem', split_axis=0, concat_axis=0, tiled=True)]
    all_to_all x9 -> x7, waiting for transfers between devices: 152 us -> 13 us  [the longest x4 9.28 us: to_tokens(): return lax.all_to_all(x, 'fsdp', split_axis=0, concat_axis=0, tiled=True)]
    ppermute x0 -> x20, waiting for transfers between devices: none -> 137 us  [the longest x15 116 us: shifted(): return lax.ppermute(x, 'mem', [(i, (i + 2 * k) % n) for i in range(n)])]
    pallas_call x0 -> x5, Pallas kernels: none -> 111 us  [the longest x1 47.8 us: per_device(): pl.pallas_call(functools.partial(memory_backward, group, pairs), grid_spe...]
    ppermute x0 -> x20, starting transfers between devices: none -> 64.8 us  [the longest x15 59.6 us: shifted(): return lax.ppermute(x, 'mem', [(i, (i + 2 * k) % n) for i in range(n)])]
    dot_general x11 -> x3, matrix products: 68.5 us -> 12 us  [the longest x2 7.59 us: dot(): return lax.dot_general(a, b, dims, preferred_element_type=F32)]
    reshape x10 -> x8, local copies, waits for them, and re-layouts: 53.6 us -> 8.34 us  [the longest x3 4.57 us: to_heads(): x = x.reshape(rows, parts, width // parts).transpose(1, 0, 2)]
    all_gather x1, waiting for transfers between devices: 28.6 us -> 0.01 us  [per_device(): full_weight = lax.all_gather(out_weight, 'fsdp', axis=0, tiled=True)]
  transfers between devices with their start and end apart: 12 -> 28, of which waited for: 6 -> 12; matrix products, arithmetic and copies ran while one was open for 31% -> 6% of each run, Pallas kernels for 0% -> 24%
where the time goes in v1:
time: 467 us; the launch traced here: 463 us
  waiting for transfers between devices  150 us (32%)
  Pallas kernels  111 us (24%)
  starting transfers between devices  91.4 us (20%)
  blocking collectives  44.1 us (9%)
  local copies, waits for them, and re-layouts  39 us (8%)
  between operations  14.4 us (3%)
  matrix products  12 us (3%)
    ppermute x15, waiting for transfers between devices, shifted(): return lax.ppermute(x, 'mem', [(i, (i + 2 * k) % n) for i in range(n)])  116 us
    ppermute x15, starting transfers between devices, shifted(): return lax.ppermute(x, 'mem', [(i, (i + 2 * k) % n) for i in range(n)])  59.6 us
    pallas_call x1, Pallas kernels, per_device(): pl.pallas_call(functools.partial(memory_backward, group, pairs), grid_spe...  47.8 us
    all_to_all x1, blocking collectives, per_device(): lax.all_to_all(partial, 'mem', split_axis=0, concat_axis=0, tiled=True)  44.1 us
    pallas_call x1, Pallas kernels, per_device(): pl.pallas_call(functools.partial(memory_forward, group, pairs), grid_spec...  42.1 us
    unnamed x63, local copies, waits for them, and re-layouts  20.4 us
    ppermute x1, waiting for transfers between devices, gather_tokens(): far = lax.ppermute(x, 'fsdp', [(i, i ^ 2) for i in range(4)])  20.4 us
    all_to_all x4, starting transfers between devices, to_tokens(): return lax.all_to_all(x, 'fsdp', split_axis=0, concat_axis=0, tiled=True)  14.7 us
  transfers between devices with their start and end apart: 28, of which 12 were waited for; matrix products, arithmetic and copies ran while one was open for 6% of the time, Pallas kernels for 24%

profile of v1, /device:TPU:0, one launch (start us, length us, event | category | flops | bytes accessed | tf_op | source)
XLA Modules:
  0.0 463.3 jit_solution(1106191109950973860)
XLA Ops:
  7.2 3.0 collective-permute-start.1
  10.2 1.9 copy.78
  12.1 3.6 all-to-all-start
  15.7 1.6 collective-permute-start.3
  19.5 20.4 %collective-permute-done.1 = bf16[256,2048]{1,0:T(8,128)(2,1)S(1)} collective-permute-done((bf16[256,2048]{1,0:T(8,128)(2,1)}, bf16[256,2048]{1,0:T(8,128)(2,1)S(1)}, u32[]{:S(2)}, u32[]{:S(2)}) %collective-permute-start.1) | collective-permute-done | bytes 1048608 | tf_op jit(solution)/shard_map/ppermute | solution.py:353
  39.9 1.9 copy.77
  42.6 2.5 broadcast_in_dim.45
  46.2 3.7 all-to-all-done
  50.0 4.1 all-to-all-start.1
  54.1 1.5 collective-permute-start.5
  55.6 2.8 collective-permute-start.6
  58.4 2.3 constant_dynamic-update-slice_fusion.2
  61.7 1.2 collective-permute-start.7
  63.0 2.4 constant_dynamic-update-slice_fusion
  65.4 4.0 convolution_convert_fusion.1.do_ref.rest_4_
  69.3 1.5 collective-permute-done.5.rest_1_
  71.6 1.4 collective-permute-start.10
  73.0 19.9 %collective-permute-done.6.rest_2_ = bf16[1024,256]{1,0:T(8,128)(2,1)S(1)} collective-permute-done((bf16[1024,256]{1,0:T(8,128)(2,1)S(1)}, bf16[1024,256]{1,0:T(8,128)(2,1)S(1)}, u32[]{:S(2)}, u32[]{:S(2)}) %collective-permute-start.6) | collective-permute-done | bytes 524320 | tf_op jit(solution)/shard_map/ppermute | solution.py:382
  93.7 21.1 %collective-permute-start.8 = (bf16[1024,256]{1,0:T(8,128)(2,1)S(1)}, bf16[1024,256]{1,0:T(8,128)(2,1)}, u32[]{:S(2)}, u32[]{:S(2)}) collective-permute-start(bf16[1024,256]{1,0:T(8,128)(2,1)S(1)} %convolution_convert_fusion.1.do_ref.rest_4_), channel_id=1, source_target_pairs={{0,8},{4,12},{8,16},{12,20},{16,24},{20,28},{24,0},{28,4},{1,9},{5... | collective-permute-start | bytes 1572872 | tf_op jit(solution)/shard_map/ppermute | solution.py:382
  115.5 3.4 collective-permute-start.9
  119.0 4.2 all-to-all-start.2
  123.7 6.8 %collective-permute-done.8.rest_5_ = bf16[1024,256]{1,0:T(8,128)(2,1)} collective-permute-done((bf16[1024,256]{1,0:T(8,128)(2,1)S(1)}, bf16[1024,256]{1,0:T(8,128)(2,1)}, u32[]{:S(2)}, u32[]{:S(2)}) %collective-permute-start.8) | collective-permute-done | bytes 524320 | tf_op jit(solution)/shard_map/ppermute | solution.py:382
  130.6 21.3 %collective-permute-done.9.rest_6_ = bf16[1024,256]{1,0:T(8,128)(2,1)} collective-permute-done((bf16[1024,256]{1,0:T(8,128)(2,1)S(1)}, bf16[1024,256]{1,0:T(8,128)(2,1)}, u32[]{:S(2)}, u32[]{:S(2)}) %collective-permute-start.9) | collective-permute-done | bytes 524320 | tf_op jit(solution)/shard_map/ppermute | solution.py:382
  151.9 1.6 copy-done.1
  156.6 42.1 %memory_forward.1 = (bf16[8,256,128]{2,1,0:T(8,128)(2,1)S(1)}, bf16[8,256,128]{2,1,0:T(8,128)(2,1)}, bf16[8,256,128]{2,1,0:T(8,128)(2,1)S(1)}, bf16[8,256,128]{2,1,0:T(8,128)(2,1)S(1)}, f32[4,8,2,512]{3,2,1,0:T(2,128)S(1)}) custom-call(s32[32]{0:T(128)S(1)} %reduce_sum.39.counts, s32[256]{0:T(256)S(1)} %reshape.271.lists, bf16[4096,256]{1,0:T(8,128)(2,1)S(1)} %copy-done, ...), custom_call_target="tpu_custom_call" | custom-call | tf_op jit(solution)/shard_map/memory_forward/pallas_call | solution.py:427
  201.1 1.4 collective-permute-start.11
  202.6 9.3 %local.1 = (f32[8,256,128]{2,1,0:T(8,128)S(1)}, f32[8,256,128]{2,1,0:T(8,128)S(1)}, bf16[1024,256]{1,0:T(8,128)(2,1)S(1)}, bf16[1024,256]{1,0:T(8,128)(2,1)S(1)}) custom-call(f32[4]{0:T(128)S(1)} %add_divide_fusion.gate, bf16[1024,256]{1,0:T(8,128)(2,1)S(1)} %bitcast.65, bf16[1024,256]{1,0:T(8,128)(2,1)} %bitcast.3.k_ref, bf16[1024,256]{1,0:T(8,128)(2,1)} %bitcast.5.v_ref, ...), custom_call_target="tpu_custom_call" | custom-call | tf_op jit(solution)/shard_map/local/pallas_call | solution.py:402
  215.5 4.1 all-to-all-start.5
  219.7 13.9 %collective-permute-start.15 = (f32[4,8,2,512]{3,2,1,0:T(2,128)S(1)}, f32[4,8,2,512]{3,2,1,0:T(2,128)S(1)}, u32[]{:S(2)}, u32[]{:S(2)}) collective-permute-start(f32[4,8,2,512]{3,2,1,0:T(2,128)S(1)} %get-tuple-element.23.rest_4_.rest_8_), channel_id=1, source_target_pairs={{0,16},{4,20},{8,24},{12,28},{16,0},{20,4},{24,8},{28,12},{1,17},{... | collective-permute-start | bytes 393224 | tf_op jit(solution)/shard_map/ppermute | solution.py:382
  233.5 1.9 collective-permute-start.16
  236.1 2.3 collective-permute-start.13
  238.4 30.3 %collective-permute-done.15.rest_6_.rest_10_ = f32[4,8,2,512]{3,2,1,0:T(2,128)S(1)} collective-permute-done((f32[4,8,2,512]{3,2,1,0:T(2,128)S(1)}, f32[4,8,2,512]{3,2,1,0:T(2,128)S(1)}, u32[]{:S(2)}, u32[]{:S(2)}) %collective-permute-start.15) | collective-permute-done | bytes 131104 | tf_op jit(solution)/shard_map/ppermute | solution.py:382
  268.7 1.6 copy-done.2
  273.5 47.8 %memory_backward.1 = (bf16[8,256,128]{2,1,0:T(8,128)(2,1)S(1)}, bf16[8,256,128]{2,1,0:T(8,128)(2,1)}, bf16[8,256,128]{2,1,0:T(8,128)(2,1)}, bf16[8,256,128]{2,1,0:T(8,128)(2,1)}) custom-call(s32[32]{0:T(128)S(1)} %reduce_sum.39.counts, s32[256]{0:T(256)S(1)} %reshape.271.lists, bf16[4096,256]{1,0:T(8,128)(2,1)S(1)} %copy-done, ...), custom_call_target="tpu_custom_call" | custom-call | tf_op jit(solution)/shard_map/memory_backward/pallas_call | solution.py:452
  322.1 8.7 %collective-permute-start.18 = (bf16[8,256,128]{2,1,0:T(8,128)(2,1)}, bf16[8,256,128]{2,1,0:T(8,128)(2,1)S(1)}, u32[]{:S(2)}, u32[]{:S(2)}) collective-permute-start(bf16[8,256,128]{2,1,0:T(8,128)(2,1)} %get-tuple-element.27), channel_id=1, source_target_pairs={{0,16},{4,20},{8,24},{12,28},{16,0},{20,4},{24,8},{28,12},{1,17},{... | collective-permute-start | bytes 1572872 | tf_op jit(solution)/shard_map/ppermute | solution.py:382
  330.8 3.5 all-to-all-start.6
  334.3 6.1 %attention.1 = bf16[1024,256]{1,0:T(8,128)(2,1)} custom-call(f32[4]{0:T(128)} %copy-done.22, f32[8,256,128]{2,1,0:T(8,128)} %copy-done.12, bf16[8,256,128]{2,1,0:T(8,128)(2,1)} %copy-done.18, bf16[8,256,128]{2,1,0:T(8,128)(2,1)} %collective-permute-done.11.rest_1_, bf16[8,256,128]{2,1,0:T(8,128)(2,1)} %collective-permute-done.12.rest_2_, ...), custom_call_target="tpu_custom_call" | custom-call | tf_op jit(solution)/shard_map/attention/pallas_call | solution.py:473
  340.4 1.2 collective-permute-done.17.rest_1_
  341.6 34.9 %collective-permute-done.18.rest_2_ = bf16[8,256,128]{2,1,0:T(8,128)(2,1)S(1)} collective-permute-done((bf16[8,256,128]{2,1,0:T(8,128)(2,1)}, bf16[8,256,128]{2,1,0:T(8,128)(2,1)S(1)}, u32[]{:S(2)}, u32[]{:S(2)}) %collective-permute-start.18) | collective-permute-done | bytes 524320 | tf_op jit(solution)/shard_map/ppermute | solution.py:382
  377.5 5.9 %query_grad.1 = bf16[1024,256]{1,0:T(8,128)(2,1)} custom-call(f32[4]{0:T(128)} %copy-done.22, f32[8,256,128]{2,1,0:T(8,128)} %copy-done.13, bf16[8,256,128]{2,1,0:T(8,128)(2,1)} %copy-done.21, bf16[8,256,128]{2,1,0:T(8,128)(2,1)} %copy-done.27, bf16[8,256,128]{2,1,0:T(8,128)(2,1)} %copy-done.28, bf16[8,256,128]{2,1,0:T(8,128)(2,1)} %copy-done.29), custom_call_target="tpu_custom_call" | custom-call | tf_op jit(solution)/shard_map/query_grad/pallas_call | solution.py:481
  383.3 3.7 all-to-all-start.4
  387.0 3.6 convolution_convert_fusion
  390.7 4.9 %all-to-all-done.4 = bf16[4,256,256]{2,1,0:T(8,128)(2,1)S(1)} async-done(((bf16[4,256,256]{2,1,0:T(8,128)(2,1)}), bf16[4,256,256]{2,1,0:T(8,128)(2,1)S(1)}, u32[]{:S(2)}, u32[]{:S(2)}) %all-to-all-start.4) | async-done | bytes 524320 | tf_op jit(solution)/shard_map/all_to_all | solution.py:339
  395.6 44.1 %all_to_all.40 = bf16[8,256,256]{2,1,0:T(8,128)(2,1)S(1)} all-to-all(bf16[8,256,256]{2,1,0:T(8,128)(2,1)S(1)} %bitcast.69), channel_id=1, replica_groups=mesh['mem'=8,'fsdp'=4] {'mem'}, dimensions={0} | all-to-all | bytes 2097152 | tf_op jit(solution)/shard_map/all_to_all | solution.py:501
  439.8 3.5 all-to-all-start.3
  443.2 1.9 copy.69
  447.7 4.4 all-to-all-done.3
  452.0 4.4 fusion
  (112 shorter events, 25.5 us)
Async XLA Ops:
  7.2 34.6 %copy-start.26 = (bf16[256,1024]{1,0:T(8,128)(2,1)S(1)}, bf16[256,1024]{1,0:T(8,128)(2,1)}, u32[]{:S(2)}) copy-start(bf16[256,1024]{1,0:T(8,128)(2,1)} %param.11) | copy-start | bytes 1572868
  7.2 32.7 %collective-permute-start.1 = (bf16[256,2048]{1,0:T(8,128)(2,1)}, bf16[256,2048]{1,0:T(8,128)(2,1)S(1)}, u32[]{:S(2)}, u32[]{:S(2)}) collective-permute-start(bf16[256,2048]{1,0:T(8,128)(2,1)} %param.17), channel_id=1, source_target_pairs={{0,2},{1,3},{2,0},{3,1},{4,6},{5,7},{6,4},{7,5},{8,10},{9,11},{10,... | collective-permute-start | bytes 3145736 | tf_op jit(solution)/shard_map/ppermute | solution.py:353
  10.2 45.4 %collective-permute-start = (bf16[256,2048]{1,0:T(8,128)(2,1)}, bf16[256,2048]{1,0:T(8,128)(2,1)}, u32[]{:S(2)}, u32[]{:S(2)}) collective-permute-start(bf16[256,2048]{1,0:T(8,128)(2,1)} %param.17), channel_id=1, source_target_pairs={{0,1},{1,0},{2,3},{3,2},{4,5},{5,4},{6,7},{7,6},{8,9},{9,8},{10,11... | collective-permute-start | bytes 3145736 | tf_op jit(solution)/shard_map/ppermute | solution.py:354
  12.1 33.1 %copy-start.25 = (bf16[256,2048]{1,0:T(8,128)(2,1)S(1)}, bf16[256,2048]{1,0:T(8,128)(2,1)}, u32[]{:S(2)}) copy-start(bf16[256,2048]{1,0:T(8,128)(2,1)} %param.17) | copy-start | bytes 3145732
  12.1 37.9 %all-to-all-start = ((bf16[4,256,256]{2,1,0:T(8,128)(2,1)}), bf16[4,256,256]{2,1,0:T(8,128)(2,1)S(1)}, u32[]{:S(2)}, u32[]{:S(2)}) async-start(bf16[4,256,256]{2,1,0:T(8,128)(2,1)} %bitcast.60), calls=%async_computation | async-start | bytes 1048576 | tf_op jit(solution)/shard_map/all_to_all | solution.py:332
  15.7 436.4 %all-gather.2.cloned.1.call-start = ((), (), s32[]{:S(2)}) async-start(), calls=%async_computation.8 | async-start | bytes 5242880 | tf_op jit(solution)/shard_map/all_gather | solution.py:395
  15.7 108.0 %collective-permute-start.3 = (bf16[4096,256]{1,0:T(8,128)(2,1)}, bf16[4096,256]{1,0:T(8,128)(2,1)}, u32[]{:S(2)}, u32[]{:S(2)}) collective-permute-start(bf16[4096,256]{1,0:T(8,128)(2,1)} %k_own.3), channel_id=1, source_target_pairs={{0,4},{4,0},{8,12},{12,8},{16,20},{20,16},{24,28},{28,24},{1,5},{5... | collective-permute-start | bytes 6291464 | tf_op jit(solution)/shard_map/ppermute | solution.py:385
  17.3 106.4 %collective-permute-start.4 = (bf16[4096,256]{1,0:T(8,128)(2,1)}, bf16[4096,256]{1,0:T(8,128)(2,1)}, u32[]{:S(2)}, u32[]{:S(2)}) collective-permute-start(bf16[4096,256]{1,0:T(8,128)(2,1)} %v_own.3), channel_id=1, source_target_pairs={{0,4},{4,0},{8,12},{12,8},{16,20},{20,16},{24,28},{28,24},{1,5},{5... | collective-permute-start | bytes 6291464 | tf_op jit(solution)/shard_map/ppermute | solution.py:386
  39.9 21.8 %collective-permute-start.2 = (bf16[256,2048]{1,0:T(8,128)(2,1)S(1)}, bf16[256,2048]{1,0:T(8,128)(2,1)}, u32[]{:S(2)}, u32[]{:S(2)}) collective-permute-start(bf16[256,2048]{1,0:T(8,128)(2,1)S(1)} %collective-permute-done.1), channel_id=1, source_target_pairs={{0,1},{1,0},{2,3},{3,2},{4,5},{5,4},{6,7},{7,6},{8,9},{9,8},{10,11... | collective-permute-start | bytes 3145736 | tf_op jit(solution)/shard_map/ppermute | solution.py:355
  50.0 69.1 %all-to-all-start.1 = ((bf16[4,256,256]{2,1,0:T(8,128)(2,1)}), bf16[4,256,256]{2,1,0:T(8,128)(2,1)}, u32[]{:S(2)}, u32[]{:S(2)}) async-start(bf16[4,256,256]{2,1,0:T(8,128)(2,1)} %bitcast.58), calls=%async_computation.1 | async-start | bytes 1048576 | tf_op jit(solution)/shard_map/all_to_all | solution.py:332
  54.1 16.7 %collective-permute-start.5 = (bf16[1024,256]{1,0:T(8,128)(2,1)S(1)}, bf16[1024,256]{1,0:T(8,128)(2,1)S(1)}, u32[]{:S(2)}, u32[]{:S(2)}) collective-permute-start(bf16[1024,256]{1,0:T(8,128)(2,1)S(1)} %bitcast.61), channel_id=1, source_target_pairs={{0,8},{4,12},{8,16},{12,20},{16,24},{20,28},{24,0},{28,4},{1,9},{5... | collective-permute-start | bytes 1572872 | tf_op jit(solution)/shard_map/ppermute | solution.py:382
  55.6 37.3 %collective-permute-start.6 = (bf16[1024,256]{1,0:T(8,128)(2,1)S(1)}, bf16[1024,256]{1,0:T(8,128)(2,1)S(1)}, u32[]{:S(2)}, u32[]{:S(2)}) collective-permute-start(bf16[1024,256]{1,0:T(8,128)(2,1)S(1)} %bitcast.62), channel_id=1, source_target_pairs={{0,16},{4,20},{8,24},{12,28},{16,0},{20,4},{24,8},{28,12},{1,17},{... | collective-permute-start | bytes 1572872 | tf_op jit(solution)/shard_map/ppermute | solution.py:382
  61.7 53.0 %collective-permute-start.7 = (bf16[1024,256]{1,0:T(8,128)(2,1)S(1)}, bf16[1024,256]{1,0:T(8,128)(2,1)S(1)}, u32[]{:S(2)}, u32[]{:S(2)}) collective-permute-start(bf16[1024,256]{1,0:T(8,128)(2,1)S(1)} %bitcast.63), channel_id=1, source_target_pairs={{0,24},{4,28},{8,0},{12,4},{16,8},{20,12},{24,16},{28,20},{1,25},{... | collective-permute-start | bytes 1572872 | tf_op jit(solution)/shard_map/ppermute | solution.py:382
  65.4 86.5 %copy-start = (bf16[4096,256]{1,0:T(8,128)(2,1)S(1)}, bf16[4096,256]{1,0:T(8,128)(2,1)}, u32[]{:S(2)}) copy-start(bf16[4096,256]{1,0:T(8,128)(2,1)} %k_own.3) | copy-start | bytes 6291460
  71.6 52.1 %collective-permute-start.10 = (bf16[1024,256]{1,0:T(8,128)(2,1)S(1)}, bf16[1024,256]{1,0:T(8,128)(2,1)}, u32[]{:S(2)}, u32[]{:S(2)}) collective-permute-start(bf16[1024,256]{1,0:T(8,128)(2,1)S(1)} %convolution_convert_fusion.1.do_ref.rest_4_), channel_id=1, source_target_pairs={{0,24},{4,28},{8,0},{12,4},{16,8},{20,12},{24,16},{28,20},{1,25},{... | collective-permute-start | bytes 1572872 | tf_op jit(solution)/shard_map/ppermute | solution.py:382
  93.7 36.9 %collective-permute-start.8 = (bf16[1024,256]{1,0:T(8,128)(2,1)S(1)}, bf16[1024,256]{1,0:T(8,128)(2,1)}, u32[]{:S(2)}, u32[]{:S(2)}) collective-permute-start(bf16[1024,256]{1,0:T(8,128)(2,1)S(1)} %convolution_convert_fusion.1.do_ref.rest_4_), channel_id=1, source_target_pairs={{0,8},{4,12},{8,16},{12,20},{16,24},{20,28},{24,0},{28,4},{1,9},{5... | collective-permute-start | bytes 1572872 | tf_op jit(solution)/shard_map/ppermute | solution.py:382
  115.5 36.3 %collective-permute-start.9 = (bf16[1024,256]{1,0:T(8,128)(2,1)S(1)}, bf16[1024,256]{1,0:T(8,128)(2,1)}, u32[]{:S(2)}, u32[]{:S(2)}) collective-permute-start(bf16[1024,256]{1,0:T(8,128)(2,1)S(1)} %convolution_convert_fusion.1.do_ref.rest_4_), channel_id=1, source_target_pairs={{0,16},{4,20},{8,24},{12,28},{16,0},{20,4},{24,8},{28,12},{1,17},{... | collective-permute-start | bytes 1572872 | tf_op jit(solution)/shard_map/ppermute | solution.py:382
  119.0 83.6 %all-to-all-start.2 = ((bf16[4,256,256]{2,1,0:T(8,128)(2,1)}), bf16[4,256,256]{2,1,0:T(8,128)(2,1)}, u32[]{:S(2)}, u32[]{:S(2)}) async-start(bf16[4,256,256]{2,1,0:T(8,128)(2,1)} %bitcast.70), calls=%async_computation.2 | async-start | bytes 1048576 | tf_op jit(solution)/shard_map/all_to_all | solution.py:332
  123.6 78.9 %copy-start.30 = (f32[16]{0:T(128)S(1)}, f32[16]{0:T(128)}, u32[]{:S(2)}) copy-start(f32[16]{0:T(128)} %param.15) | copy-start | bytes 196
  151.9 1.6 copy-start.1
  153.5 1.0 copy-start.4
  154.5 1.0 copy-start.7
  155.5 1.0 copy-start.10
  201.1 120.2 %copy-start.14 = (f32[4,8,2,512]{3,2,1,0:T(2,128)}, f32[4,8,2,512]{3,2,1,0:T(2,128)S(1)}, u32[]{:S(2)}) copy-start(f32[4,8,2,512]{3,2,1,0:T(2,128)S(1)} %get-tuple-element.23.rest_4_.rest_8_) | copy-start | bytes 393220
  201.1 129.7 %collective-permute-start.11 = (bf16[8,256,128]{2,1,0:T(8,128)(2,1)}, bf16[8,256,128]{2,1,0:T(8,128)(2,1)}, u32[]{:S(2)}, u32[]{:S(2)}) collective-permute-start(bf16[8,256,128]{2,1,0:T(8,128)(2,1)} %get-tuple-element.20), channel_id=1, source_target_pairs={{0,24},{4,28},{8,0},{12,4},{16,8},{20,12},{24,16},{28,20},{1,25},{... | collective-permute-start | bytes 1572872 | tf_op jit(solution)/shard_map/ppermute | solution.py:382
  202.6 118.7 %copy-start.22 = (f32[4]{0:T(128)}, f32[4]{0:T(128)S(1)}, u32[]{:S(2)}) copy-start(f32[4]{0:T(128)S(1)} %add_divide_fusion.gate) | copy-start | bytes 52
  211.9 1.0 copy-start.12
  212.9 1.0 copy-start.13
  215.5 115.3 %all-to-all-start.5 = ((bf16[4,256,256]{2,1,0:T(8,128)(2,1)}), bf16[4,256,256]{2,1,0:T(8,128)(2,1)}, u32[]{:S(2)}, u32[]{:S(2)}) async-start(bf16[4,256,256]{2,1,0:T(8,128)(2,1)} %bitcast.68), calls=%async_computation.5 | async-start | bytes 1048576 | tf_op jit(solution)/shard_map/all_to_all | solution.py:339
  219.6 16.4 %collective-permute-start.14 = (f32[4,8,2,512]{3,2,1,0:T(2,128)S(1)}, f32[4,8,2,512]{3,2,1,0:T(2,128)S(1)}, u32[]{:S(2)}, u32[]{:S(2)}) collective-permute-start(f32[4,8,2,512]{3,2,1,0:T(2,128)S(1)} %get-tuple-element.23.rest_4_.rest_8_), channel_id=1, source_target_pairs={{0,24},{4,28},{8,0},{12,4},{16,8},{20,12},{24,16},{28,20},{1,25},{... | collective-permute-start | bytes 393224 | tf_op jit(solution)/shard_map/ppermute | solution.py:382
  219.7 49.0 %collective-permute-start.15 = (f32[4,8,2,512]{3,2,1,0:T(2,128)S(1)}, f32[4,8,2,512]{3,2,1,0:T(2,128)S(1)}, u32[]{:S(2)}, u32[]{:S(2)}) collective-permute-start(f32[4,8,2,512]{3,2,1,0:T(2,128)S(1)} %get-tuple-element.23.rest_4_.rest_8_), channel_id=1, source_target_pairs={{0,16},{4,20},{8,24},{12,28},{16,0},{20,4},{24,8},{28,12},{1,17},{... | collective-permute-start | bytes 393224 | tf_op jit(solution)/shard_map/ppermute | solution.py:382
  233.5 35.2 %collective-permute-start.16 = (f32[4,8,2,512]{3,2,1,0:T(2,128)S(1)}, f32[4,8,2,512]{3,2,1,0:T(2,128)S(1)}, u32[]{:S(2)}, u32[]{:S(2)}) collective-permute-start(f32[4,8,2,512]{3,2,1,0:T(2,128)S(1)} %get-tuple-element.23.rest_4_.rest_8_), channel_id=1, source_target_pairs={{0,8},{4,12},{8,16},{12,20},{16,24},{20,28},{24,0},{28,4},{1,9},{5... | collective-permute-start | bytes 393224 | tf_op jit(solution)/shard_map/ppermute | solution.py:382
  235.5 98.8 %collective-permute-start.12 = (bf16[8,256,128]{2,1,0:T(8,128)(2,1)}, bf16[8,256,128]{2,1,0:T(8,128)(2,1)}, u32[]{:S(2)}, u32[]{:S(2)}) collective-permute-start(bf16[8,256,128]{2,1,0:T(8,128)(2,1)} %copy-done.24), channel_id=1, source_target_pairs={{0,16},{4,20},{8,24},{12,28},{16,0},{20,4},{24,8},{28,12},{1,17},{... | collective-permute-start | bytes 1572872 | tf_op jit(solution)/shard_map/ppermute | solution.py:382
  236.0 85.2 %copy-start.15 = (f32[4,8,2,512]{3,2,1,0:T(2,128)}, f32[4,8,2,512]{3,2,1,0:T(2,128)S(1)}, u32[]{:S(2)}) copy-start(f32[4,8,2,512]{3,2,1,0:T(2,128)S(1)} %collective-permute-done.14.rest_5_.rest_11_) | copy-start | bytes 393220
  236.1 98.3 %collective-permute-start.13 = (bf16[8,256,128]{2,1,0:T(8,128)(2,1)}, bf16[8,256,128]{2,1,0:T(8,128)(2,1)}, u32[]{:S(2)}, u32[]{:S(2)}) collective-permute-start(bf16[8,256,128]{2,1,0:T(8,128)(2,1)} %copy-done.23), channel_id=1, source_target_pairs={{0,8},{4,12},{8,16},{12,20},{16,24},{20,28},{24,0},{28,4},{1,9},{5... | collective-permute-start | bytes 1572872 | tf_op jit(solution)/shard_map/ppermute | solution.py:382
  268.7 52.6 %copy-start.16 = (f32[4,8,2,512]{3,2,1,0:T(2,128)}, f32[4,8,2,512]{3,2,1,0:T(2,128)S(1)}, u32[]{:S(2)}) copy-start(f32[4,8,2,512]{3,2,1,0:T(2,128)S(1)} %collective-permute-done.15.rest_6_.rest_10_) | copy-start | bytes 393220
  268.7 1.6 copy-start.2
  270.3 1.0 copy-start.5
  271.4 1.0 copy-start.8
  272.4 1.0 copy-start.11
  273.5 47.9 %copy-start.17 = (f32[4,8,2,512]{3,2,1,0:T(2,128)}, f32[4,8,2,512]{3,2,1,0:T(2,128)S(1)}, u32[]{:S(2)}) copy-start(f32[4,8,2,512]{3,2,1,0:T(2,128)S(1)} %collective-permute-done.16.rest_7_.rest_9_) | copy-start | bytes 393220
  322.1 19.5 %collective-permute-start.17 = (bf16[8,256,128]{2,1,0:T(8,128)(2,1)}, bf16[8,256,128]{2,1,0:T(8,128)(2,1)S(1)}, u32[]{:S(2)}, u32[]{:S(2)}) collective-permute-start(bf16[8,256,128]{2,1,0:T(8,128)(2,1)} %get-tuple-element.26), channel_id=1, source_target_pairs={{0,24},{4,28},{8,0},{12,4},{16,8},{20,12},{24,16},{28,20},{1,25},{... | collective-permute-start | bytes 1572872 | tf_op jit(solution)/shard_map/ppermute | solution.py:382
  322.1 54.4 %collective-permute-start.18 = (bf16[8,256,128]{2,1,0:T(8,128)(2,1)}, bf16[8,256,128]{2,1,0:T(8,128)(2,1)S(1)}, u32[]{:S(2)}, u32[]{:S(2)}) collective-permute-start(bf16[8,256,128]{2,1,0:T(8,128)(2,1)} %get-tuple-element.27), channel_id=1, source_target_pairs={{0,16},{4,20},{8,24},{12,28},{16,0},{20,4},{24,8},{28,12},{1,17},{... | collective-permute-start | bytes 1572872 | tf_op jit(solution)/shard_map/ppermute | solution.py:382
  330.8 45.7 %collective-permute-start.19 = (bf16[8,256,128]{2,1,0:T(8,128)(2,1)}, bf16[8,256,128]{2,1,0:T(8,128)(2,1)S(1)}, u32[]{:S(2)}, u32[]{:S(2)}) collective-permute-start(bf16[8,256,128]{2,1,0:T(8,128)(2,1)} %get-tuple-element.28), channel_id=1, source_target_pairs={{0,8},{4,12},{8,16},{12,20},{16,24},{20,28},{24,0},{28,4},{1,9},{5... | collective-permute-start | bytes 1572872 | tf_op jit(solution)/shard_map/ppermute | solution.py:382
  330.8 52.5 %all-to-all-start.6 = ((bf16[4,256,256]{2,1,0:T(8,128)(2,1)}), bf16[4,256,256]{2,1,0:T(8,128)(2,1)S(1)}, u32[]{:S(2)}, u32[]{:S(2)}) async-start(bf16[4,256,256]{2,1,0:T(8,128)(2,1)} %bitcast.67), calls=%async_computation.6 | async-start | bytes 1048576 | tf_op jit(solution)/shard_map/all_to_all | solution.py:339
  341.6 34.9 %copy-start.27 = (bf16[8,256,128]{2,1,0:T(8,128)(2,1)}, bf16[8,256,128]{2,1,0:T(8,128)(2,1)S(1)}, u32[]{:S(2)}) copy-start(bf16[8,256,128]{2,1,0:T(8,128)(2,1)S(1)} %collective-permute-done.17.rest_1_) | copy-start | bytes 1572868
  383.3 12.3 %all-to-all-start.4 = ((bf16[4,256,256]{2,1,0:T(8,128)(2,1)}), bf16[4,256,256]{2,1,0:T(8,128)(2,1)S(1)}, u32[]{:S(2)}, u32[]{:S(2)}) async-start(bf16[4,256,256]{2,1,0:T(8,128)(2,1)} %bitcast.73), calls=%async_computation.4 | async-start | bytes 1048576 | tf_op jit(solution)/shard_map/all_to_all | solution.py:339
  439.8 12.3 %all-to-all-start.3 = ((bf16[4,256,256]{2,1,0:T(8,128)(2,1)}), bf16[4,256,256]{2,1,0:T(8,128)(2,1)S(1)}, u32[]{:S(2)}, u32[]{:S(2)}) async-start(bf16[4,256,256]{2,1,0:T(8,128)(2,1)} %bitcast.10), calls=%async_computation.3 | async-start | bytes 1048576 | tf_op jit(solution)/shard_map/all_to_all | solution.py:339
  (11 other events, 8.9 us)
Sparse Core Ops, SparseCore 0:
  18.1 49.2 all-gather.1

commit v2 on v1

v2 whole, which is shorter than its diff:
```python
import functools

import jax
import jax.numpy as jnp
from jax import lax
from jax.experimental import pallas as pl
from jax.experimental.pallas import tpu as pltpu
from jax.sharding import PartitionSpec as P

DH = 64
QBLK = 128
MBLK = 128
LOW = -1e30
UNROLL = 4
HALVES = 1
SCALE = DH ** (-0.5)
BF = jnp.bfloat16
F32 = jnp.float32
NT = (((1,), (1,)), ((), ()))
NN = (((1,), (0,)), ((), ()))
TN = (((0,), (0,)), ((), ()))


def dot(a, b, dims):
    return lax.dot_general(a, b, dims, preferred_element_type=F32)


def spread(x):
    zero = jnp.zeros((DH, QBLK), x.dtype)
    upper = jnp.concatenate([x[:DH], zero], axis=1)
    lower = jnp.concatenate([zero, x[DH:]], axis=1)
    return jnp.concatenate([upper, lower], axis=0)


def query_block(ref, b, t):
    per = ref.shape[2] // QBLK
    return ref[b // per, t * 128 : (t + 1) * 128, (b % per) * QBLK : (b % per + 1) * QBLK]


def folded(x, op):
    return op(x.reshape(x.shape[0] // 8, 8, x.shape[1]), axis=0)


def own_blocks(parts):
    rows = []
    for part in parts:
        rows.append(part[:DH, :QBLK])
        rows.append(part[DH:, QBLK:])
    return rows


def at_slot(slot, last, column=0):
    def index(s, b, *_):
        return (jnp.where(s == slot, b, jnp.where(s > slot, last, 0)), column, 0)

    return index


def start_step(group, pairs, half, slot, memory, buffers, sems, q_refs, do_refs, q_t, do_t):
    rows, width = buffers[0].shape
    rows = rows // 2
    blocks = q_t.shape[0] - 1

    @pl.when((slot == 0) & (pl.program_id(1) == 0))
    def _():
        own = pl.ds(half * width, width)
        sources = [memory[0].at[:, own], memory[1], memory[2].at[:, own], memory[3]]
        targets = [buffers[i].at[pl.ds(j * rows, rows)] for i in range(2) for j in range(2)]
        copies = [
            pltpu.make_async_copy(source, target, sems.at[i])
            for i, (source, target) in enumerate(zip(sources, targets))
        ]
        for copy in copies:
            copy.start()
        q_t[...] = jnp.zeros_like(q_t)
        do_t[...] = jnp.zeros_like(do_t)
        for copy in copies:
            copy.wait()

    for i in range(group):

        @pl.when(slot == i)
        def _():
            for b in range(blocks):
                for t in range(pairs):
                    for refs, out in ((q_refs, q_t), (do_refs, do_t)):
                        x = query_block(refs[i], b, t)
                        out[b, t, :DH, :QBLK] = x[:DH]
                        out[b, t, DH:, QBLK:] = x[DH:]


def memory_forward(
    group, pairs, half, counts, places, homes, k_own, k_par, v_own, v_par, *rest
):
    q_refs = rest[:group]
    do_refs = rest[group : 2 * group]
    o_refs = rest[2 * group : 3 * group]
    stat_ref = rest[3 * group]
    kbuf, vbuf, q_t, do_t, scores, tops, norms, means, acc, sems = rest[3 * group + 1 :]
    slot = pl.program_id(0)
    number = slot * pl.num_programs(1) + pl.program_id(1)
    cap = scores.shape[0]
    blocks = q_t.shape[0] - 1
    start_step(
        group, pairs, half, slot, (k_own, k_par, v_own, v_par), (kbuf, vbuf), sems,
        q_refs, do_refs, q_t, do_t,
    )
    tops[...] = jnp.full(tops.shape, LOW, F32)
    norms[...] = jnp.zeros_like(norms)
    means[...] = jnp.zeros_like(means)
    acc[...] = jnp.zeros_like(acc)
    turns = (counts[number] + UNROLL - 1) // UNROLL

    def first(turn, carry):
        found = []
        for u in range(UNROLL):
            j = turn * UNROLL + u
            row = pl.multiple_of(places[number * cap + j] * MBLK, MBLK)
            b = homes[number * cap + j]
            for t in range(pairs):
                cols = slice(t * 128, (t + 1) * 128)
                s = dot(kbuf[pl.ds(row, MBLK), cols], q_t[b, t], NN)
                scores[j, t] = s
                found.append((b, t, folded(s, jnp.max)))
        for b, t, top in found:
            tops[b, t] = jnp.maximum(tops[b, t], top)
        return carry

    lax.fori_loop(0, turns, first, 0)
    tops[...] = jnp.broadcast_to(jnp.max(tops[...], axis=2, keepdims=True), tops.shape)

    def second(turn, carry):
        found = []
        for u in range(UNROLL):
            j = turn * UNROLL + u
            row = pl.multiple_of(places[number * cap + j] * MBLK, MBLK)
            b = homes[number * cap + j]
            for t in range(pairs):
                cols = slice(t * 128, (t + 1) * 128)
                values = vbuf[pl.ds(row, MBLK), cols]
                slope = dot(values, do_t[b, t], NN)
                p = jnp.exp(scores[j, t] - tops[b, t, 0:1, :])
                found.append(
                    (b, t, folded(p, jnp.sum), folded(p * slope, jnp.sum),
                     dot(values, p.astype(BF), TN))
                )
        for b, t, norm, mean, o in found:
            norms[b, t] += norm
            means[b, t] += mean
            acc[b, t] += o
        return carry

    lax.fori_loop(0, turns, second, 0)
    results = []
    for b in range(blocks):
        parts = []
        for t in range(pairs):
            wide = slice(t * 256, (t + 1) * 256)
            norm = jnp.sum(norms[b, t], axis=0, keepdims=True)
            mean = jnp.sum(means[b, t], axis=0, keepdims=True)
            some = norm > 0.0
            safe = jnp.where(some, norm, 1.0)
            inverse = 1.0 / safe
            lse = jnp.where(some, tops[b, t, 0:1, :] + jnp.log(safe), LOW)
            stat_ref[0, b, 0:1, wide] = lse
            stat_ref[0, b, 1:2, wide] = mean * inverse
            parts.append(acc[b, t] * inverse)
        results.append(jnp.concatenate(own_blocks(parts), axis=0).astype(BF))
    for i in range(group):

        @pl.when(slot == i)
        def _():
            for b in range(blocks):
                o_refs[i][b] = results[b]


def merged(stat_refs, b):
    lses = [ref[0, b, 0:1, :] for ref in stat_refs]
    top = functools.reduce(jnp.maximum, lses)
    shares = [jnp.exp(x - top) for x in lses]
    norm = functools.reduce(jnp.add, shares)
    return top, shares, norm


def memory_backward(
    group, pairs, half, counts, places, homes, k_own, k_par, v_own, v_par, *rest
):
    q_refs = rest[:group]
    do_refs = rest[group : 2 * group]
    stat_refs = rest[2 * group : 3 * group]
    dq_refs = rest[3 * group : 4 * group]
    kbuf, vbuf, q_t, do_t, weights, lses, means, acc, sems = rest[4 * group :]
    slot = pl.program_id(0)
    number = slot * pl.num_programs(1) + pl.program_id(1)
    cap = places.shape[0] // counts.shape[0]
    blocks = q_t.shape[0] - 1
    start_step(
        group, pairs, half, slot, (k_own, k_par, v_own, v_par), (kbuf, vbuf), sems,
        q_refs, do_refs, q_t, do_t,
    )
    lses[...] = jnp.zeros_like(lses)
    means[...] = jnp.zeros_like(means)
    for b in range(blocks):
        top, shares, norm = merged(stat_refs, b)
        lse = top + jnp.log(norm)
        mean = functools.reduce(
            jnp.add, [x * ref[0, b, 1:2, :] for x, ref in zip(shares, stat_refs)]
        ) / norm
        for t in range(pairs):
            wide = slice(t * 256, (t + 1) * 256)
            lses[b, t] = lse[:, wide]
            means[b, t] = mean[:, wide]
    acc[...] = jnp.zeros_like(acc)

    turns = (counts[number] + UNROLL - 1) // UNROLL

    def first(turn, carry):
        for u in range(UNROLL):
            j = turn * UNROLL + u
            row = pl.multiple_of(places[number * cap + j] * MBLK, MBLK)
            b = homes[number * cap + j]
            for t in range(pairs):
                cols = slice(t * 128, (t + 1) * 128)
                s = dot(kbuf[pl.ds(row, MBLK), cols], q_t[b, t], NN)
                weights[j, t] = jnp.exp(s - lses[b, t])
        return carry

    lax.fori_loop(0, turns, first, 0)

    def second(turn, carry):
        found = []
        for u in range(UNROLL):
            j = turn * UNROLL + u
            row = pl.multiple_of(places[number * cap + j] * MBLK, MBLK)
            b = homes[number * cap + j]
            for t in range(pairs):
                cols = slice(t * 128, (t + 1) * 128)
                slope = dot(vbuf[pl.ds(row, MBLK), cols], do_t[b, t], NN)
                delta = weights[j, t] * (slope - means[b, t])
                found.append((b, t, dot(kbuf[pl.ds(row, MBLK), cols], delta.astype(BF), TN)))
        for b, t, dq in found:
            acc[b, t] += dq
        return carry

    lax.fori_loop(0, turns, second, 0)
    results = [
        jnp.concatenate(own_blocks([acc[b, t] for t in range(pairs)]), axis=0).astype(BF)
        for b in range(blocks)
    ]
    for i in range(group):

        @pl.when(slot == i)
        def _():
            for b in range(blocks):
                dq_refs[i][b] = results[b]


def local_kernel(pairs, blocks, halves, gate, q_ref, k_ref, v_ref, *rest):
    do_refs = rest[:halves]
    o_ref, dq_ref, dk_ref, dv_ref, dk_acc, dv_acc = rest[halves:]
    per_half = pairs // halves
    dk_acc[...] = jnp.zeros_like(dk_acc)
    dv_acc[...] = jnp.zeros_like(dv_acc)
    key_at = lax.broadcasted_iota(jnp.int32, (MBLK, 2 * QBLK), 0)
    query_at = lax.broadcasted_iota(jnp.int32, (MBLK, 2 * QBLK), 1) % QBLK
    causal = key_at <= query_at
    lane = lax.broadcasted_iota(jnp.int32, (1, 128), 1)
    shares = []
    for t in range(pairs):
        shares.append(jnp.where(lane < DH, 1.0 - gate[2 * t], 1.0 - gate[2 * t + 1]))
    for t in range(pairs):
        cols = slice(t * 128, (t + 1) * 128)
        for b in range(blocks):
            q = spread(query_block(q_ref, b, t))
            do = spread(query_block(do_refs[t // per_half], b, t % per_half))
            scores, slopes = [], []
            for n in range(b + 1):
                rows = slice(n * MBLK, (n + 1) * MBLK)
                s = dot(k_ref[rows, cols], q, NN)
                scores.append(jnp.where(causal, s, LOW) if n == b else s)
                slopes.append(dot(v_ref[rows, cols], do, NN))
            largest = functools.reduce(jnp.maximum, [folded(s, jnp.max) for s in scores])
            largest = jnp.max(largest, axis=0, keepdims=True)
            weights = [jnp.exp(s - largest) for s in scores]
            norm = functools.reduce(jnp.add, [folded(p, jnp.sum) for p in weights])
            inverse = 1.0 / jnp.sum(norm, axis=0, keepdims=True)
            weights = [p * inverse for p in weights]
            mean = functools.reduce(
                jnp.add, [folded(p * x, jnp.sum) for p, x in zip(weights, slopes)]
            )
            mean = jnp.sum(mean, axis=0, keepdims=True)
            o = jnp.zeros((128, 256), F32)
            dq = jnp.zeros((128, 256), F32)
            for n in range(b + 1):
                rows = slice(n * MBLK, (n + 1) * MBLK)
                w = weights[n].astype(BF)
                delta = (weights[n] * (slopes[n] - mean)).astype(BF)
                o += dot(v_ref[rows, cols], w, TN)
                dq += dot(k_ref[rows, cols], delta, TN)
                dv_acc[rows, cols] += dot(w, do, NT)
                dk_acc[rows, cols] += dot(delta, q, NT)
            o_pair, dq_pair = own_blocks([o]), own_blocks([dq])
            for i in range(2):
                share = 1.0 - gate[2 * t + i]
                at = slice((2 * t + i) * DH, (2 * t + i + 1) * DH)
                o_ref[b, at, :] = o_pair[i] * share
                dq_ref[b, at, :] = dq_pair[i] * (share * SCALE)
        dk_ref[:, cols] = (dk_acc[:, cols] * shares[t]).astype(BF)
        dv_ref[:, cols] = (dv_acc[:, cols] * shares[t]).astype(BF)


def attention_kernel(group, heads, first, gate, local_ref, *rest):
    o_refs = rest[:group]
    stat_refs = rest[group : 2 * group]
    out_ref, out_t_ref = rest[2 * group :]
    for b in range(local_ref.shape[0]):
        _, shares, norm = merged(stat_refs, b)
        rows = []
        for h in range(heads):
            at = slice(h * DH, (h + 1) * DH)
            wide = slice(h * QBLK, (h + 1) * QBLK)
            total = functools.reduce(
                jnp.add,
                [x[:, wide] * ref[b, at, :].astype(F32) for x, ref in zip(shares, o_refs)],
            )
            rows.append(total * (gate[first + h] / norm[:, wide]) + local_ref[b, at, :])
        result = jnp.concatenate(rows, axis=0).astype(BF)
        out_t_ref[:, b * QBLK : (b + 1) * QBLK] = result
        out_ref[b * QBLK : (b + 1) * QBLK, :] = result.T


def query_grad_kernel(group, heads, first, gate, local_ref, *rest):
    dq_refs = rest[:group]
    out_ref = rest[group]
    for b in range(local_ref.shape[0]):
        rows = []
        for h in range(heads):
            at = slice(h * DH, (h + 1) * DH)
            total = functools.reduce(jnp.add, [ref[b, at, :].astype(F32) for ref in dq_refs])
            rows.append(total * (gate[first + h] * SCALE) + local_ref[b, at, :])
        result = jnp.concatenate(rows, axis=0).astype(BF)
        out_ref[b * QBLK : (b + 1) * QBLK, :] = result.T


def attention_grad_kernel(order, weight_ref, *rest):
    part_refs, out_refs = rest[:4], rest[4:]
    for i in range(4):
        grad = dot(weight_ref[...], part_refs[i][...], NT).astype(BF)
        rows = grad.shape[0] // len(out_refs)
        for j, out_ref in enumerate(out_refs):
            out_ref[order[i]] = grad[j * rows : (j + 1) * rows]


def weight_grad_kernel(order, dests, attention_ref, *rest):
    part_refs, (send_ref, keep_ref) = rest[:4], rest[4:]
    tokens = part_refs[0].shape[0]
    total = None
    for i in range(4):
        at = pl.multiple_of(order[i] * tokens, tokens)
        term = dot(attention_ref[:, pl.ds(at, tokens)], part_refs[i][...], NN)
        total = term if total is None else total + term

    @pl.when(pl.program_id(0) == 0)
    def _():
        send_ref[0] = total.astype(BF)

    @pl.when(pl.program_id(0) == 1)
    def _():
        keep_ref[0] = total.astype(BF)


ANY = pl.BlockSpec(memory_space=pl.ANY)
SMEM = pl.BlockSpec(memory_space=pltpu.SMEM)


def block_lists(block_ids, me, group, seg_dev, per_dev, cap):
    segments, per_seg, retr = block_ids.shape
    asked = per_seg * retr
    z = me // 2
    ids = block_ids.reshape(segments // (2 * seg_dev), 2, seg_dev, asked)
    ids = lax.dynamic_index_in_dim(ids, me % 2, 1, keepdims=False)
    slots = (z - jnp.arange(group, dtype=jnp.int32)) % group
    ids = jnp.take(ids, slots, axis=0).reshape(group * seg_dev, asked)
    owners = ids // per_dev
    here = owners // 2 == z
    place = ids - owners * per_dev + jnp.where(owners == me, 0, per_dev)
    position = jnp.arange(asked, dtype=jnp.int32)
    before = (position[None, :] < position[:, None])[None]
    rank = jnp.sum(jnp.logical_and(before, here[:, None, :]), axis=-1)
    chosen = jnp.logical_and(
        here[:, :, None], rank[:, :, None] == jnp.arange(cap, dtype=jnp.int32)
    )
    places = jnp.sum(jnp.where(chosen, place[:, :, None], 0), axis=1)
    home = position // retr - per_seg
    homes = per_seg + jnp.sum(jnp.where(chosen, home[None, :, None], 0), axis=1)
    counts = jnp.sum(here, axis=-1)
    return (
        counts.astype(jnp.int32),
        places.astype(jnp.int32).reshape(-1),
        homes.astype(jnp.int32).reshape(-1),
    )


def side_by_side(x):
    parts, rows, width = x.shape
    return x.transpose(1, 0, 2).reshape(rows, parts * width)


def gather_tokens(x):
    far = lax.ppermute(x, "fsdp", [(i, i ^ 2) for i in range(4)])
    near = lax.ppermute(x, "fsdp", [(i, i ^ 1) for i in range(4)])
    both = lax.ppermute(far, "fsdp", [(i, i ^ 1) for i in range(4)])
    return [x, near, far, both]


def weight_grad_plain(attention, parts, order):
    n = lax.axis_size("mem")
    rows = parts[0].shape[0]
    total = 0.0
    for i, part in enumerate(parts):
        own = lax.dynamic_slice_in_dim(attention, order[i] * rows, rows, 0)
        total = total + dot(own, part, TN)
    pieces = total.astype(BF).reshape(total.shape[0], n, -1).transpose(1, 0, 2)
    pieces = lax.all_to_all(pieces, "mem", split_axis=0, concat_axis=0, tiled=True)
    return jnp.sum(pieces.astype(F32), axis=0)


def after(first, *rest):
    return lax.optimization_barrier((first,) + rest)[1:]


def per_device(
    queries, keys, values, mem_keys, mem_values, block_ids, gate_bias, out_weight, cotangent
):
    n = lax.axis_size("mem")
    me = lax.axis_index("mem")
    fs = lax.axis_index("fsdp")
    group = n // 2
    full = mem_keys.shape[1]
    all_heads = full // DH
    width = full // HALVES
    heads = width // DH
    pairs = heads // 2
    segments, per_seg, retr = block_ids.shape
    seg_dev = segments // n
    per_dev = mem_keys.shape[0] // MBLK
    blocks = seg_dev * per_seg
    tokens = blocks * QBLK
    seg_len = per_seg * QBLK
    rows = queries.shape[0]
    seg_rows = seg_len // rows
    gating = jax.nn.sigmoid(lax.dynamic_slice_in_dim(gate_bias, fs * all_heads, all_heads))
    halves = range(HALVES)

    def shifted(x, k):
        return lax.ppermute(x, "mem", [(i, (i + 2 * k) % n) for i in range(n)])

    def exchange(x):
        return lax.all_to_all(x, "fsdp", split_axis=0, concat_axis=0, tiled=True)

    swap = [(i, i ^ 1) for i in range(n)]
    cap = -(-4 * max(1, retr * per_seg // n) // UNROLL) * UNROLL
    lists = block_lists(block_ids, me, group, seg_dev, per_dev, cap)

    par_keys, par_values = [], []
    for i in halves:
        k_part = mem_keys[:, i * width : (i + 1) * width]
        v_part = mem_values[:, i * width : (i + 1) * width]
        if i:
            (k_part,) = after(par_keys[-1], k_part)
            (v_part,) = after(par_values[-1], v_part)
        par_keys.append(lax.ppermute(k_part, "mem", swap))
        par_values.append(lax.ppermute(v_part, "mem", swap))

    q = exchange((queries * BF(SCALE)).T.reshape(4, full, rows))
    q_slots = [q] + [shifted(q, k) for k in range(1, group)]
    (cotangent,) = after(q, cotangent)
    cot_parts = gather_tokens(cotangent)
    order = fs ^ jnp.arange(4, dtype=jnp.int32)
    whole = pl.BlockSpec(memory_space=pltpu.VMEM)
    do_parts = pl.pallas_call(
        attention_grad_kernel,
        in_specs=[SMEM] + [whole] * 5,
        out_specs=[whole] * HALVES,
        out_shape=[jax.ShapeDtypeStruct((4, width, rows), BF)] * HALVES,
        compiler_params=pltpu.CompilerParams(vmem_limit_bytes=24 * 2**20),
        name="attention_grad",
    )(order, out_weight, *cot_parts)
    do_slots = [[x] + [shifted(x, k) for k in range(1, group)] for x in do_parts]
    keys, values = after(do_parts[0], keys, values)
    k, v = (
        exchange(x.reshape(rows, 4, full).transpose(1, 0, 2)).reshape(tokens, full)
        for x in (keys, values)
    )
    (late_weight,) = after(v, out_weight)
    full_weight = lax.all_gather(late_weight, "fsdp", axis=0, tiled=True)

    seg_spec = pl.BlockSpec((seg_len, full), lambda s: (s, 0))
    q_spec = pl.BlockSpec((seg_rows, full, rows), lambda s: (s, 0, 0))
    do_spec = pl.BlockSpec((seg_rows, width, rows), lambda s: (s, 0, 0))
    part_spec = pl.BlockSpec((per_seg, full, QBLK), lambda s: (s, 0, 0))
    part_shape = jax.ShapeDtypeStruct((blocks, full, QBLK), F32)
    head_shape = jax.ShapeDtypeStruct((tokens, full), BF)
    o_local, dq_local, dk, dv = pl.pallas_call(
        functools.partial(local_kernel, all_heads // 2, per_seg, HALVES),
        grid=(seg_dev,),
        in_specs=[SMEM, q_spec, seg_spec, seg_spec] + [do_spec] * HALVES,
        out_specs=[part_spec, part_spec, seg_spec, seg_spec],
        out_shape=[part_shape, part_shape, head_shape, head_shape],
        scratch_shapes=[pltpu.VMEM((seg_len, full), F32)] * 2,
        compiler_params=pltpu.CompilerParams(vmem_limit_bytes=32 * 2**20),
        name="local",
    )(gating, q, k, v, *do_parts)

    t_specs = [
        pl.BlockSpec((per_seg, width, QBLK), at_slot(i, seg_dev - 1)) for i in range(group)
    ]
    t_shape = jax.ShapeDtypeStruct((blocks, width, QBLK), BF)
    stat_block = (1, per_seg, 2, heads * QBLK)
    memory_rows = 2 * mem_keys.shape[0]
    scratch = [pltpu.VMEM((memory_rows, width), BF)] * 2
    scratch += [pltpu.VMEM((per_seg + 1, pairs, 128, 256), BF)] * 2
    scratch += [pltpu.VMEM((cap, pairs, MBLK, 256), F32)]
    acc = pltpu.VMEM((per_seg + 1, pairs, 128, 256), F32)
    rows8 = pltpu.VMEM((per_seg + 1, pairs, 8, 256), F32)
    rows1 = pltpu.VMEM((per_seg + 1, pairs, 1, 256), F32)
    sems = pltpu.SemaphoreType.DMA((4,))
    limit = pltpu.CompilerParams(vmem_limit_bytes=40 * 2**20)
    stat_specs = [
        pl.BlockSpec(stat_block, lambda s, b, *_, k=k: ((s - k) % group, b, 0, 0))
        for k in range(group)
    ]

    def slot_specs(half):
        return [
            pl.BlockSpec((seg_rows, width, rows), at_slot(i, seg_dev - 1, half))
            for i in range(group)
        ]

    o_home, stat_slots = [], []
    for i in halves:
        outs = pl.pallas_call(
            functools.partial(memory_forward, group, pairs, i),
            grid_spec=pltpu.PrefetchScalarGridSpec(
                num_scalar_prefetch=3,
                grid=(group, seg_dev),
                in_specs=[ANY] * 4 + slot_specs(i) + slot_specs(0),
                out_specs=t_specs + [pl.BlockSpec(stat_block, lambda s, b, *_: (s, b, 0, 0))],
                scratch_shapes=scratch + [rows8, rows8, rows8, acc, sems],
            ),
            out_shape=[t_shape] * group
            + [jax.ShapeDtypeStruct((group, blocks, 2, heads * QBLK), F32)],
            compiler_params=limit,
            name="memory_forward",
        )(*lists, mem_keys, par_keys[i], mem_values, par_values[i], *q_slots, *do_slots[i])
        stats = outs[group]
        stat_slots.append([stats] + [shifted(stats, k) for k in range(1, group)])
        o_home.append([outs[0]] + [shifted(outs[k], -k) for k in range(1, group)])

    dq_home = []
    last = stat_slots[-1][0]
    for i in halves:
        first_stats = after(last, *stat_slots[i])
        dq_slots = pl.pallas_call(
            functools.partial(memory_backward, group, pairs, i),
            grid_spec=pltpu.PrefetchScalarGridSpec(
                num_scalar_prefetch=3,
                grid=(group, seg_dev),
                in_specs=[ANY] * 4 + slot_specs(i) + slot_specs(0) + stat_specs,
                out_specs=t_specs,
                scratch_shapes=scratch + [rows1, rows1, acc, sems],
            ),
            out_shape=[t_shape] * group,
            compiler_params=limit,
            name="memory_backward",
        )(
            *lists, mem_keys, par_keys[i], mem_values, par_values[i],
            *q_slots, *do_slots[i], *first_stats,
        )
        last = dq_slots[0]
        dq_home.append([dq_slots[0]] + [shifted(dq_slots[k], -k) for k in range(1, group)])

    home_spec = pl.BlockSpec((per_seg, width, QBLK), lambda b: (b, 0, 0))
    home_out = pl.BlockSpec((seg_len, width), lambda b: (b, 0))
    home_shape = jax.ShapeDtypeStruct((tokens, width), BF)
    home_specs = [
        pl.BlockSpec(stat_block, lambda b, k=k: (k, b, 0, 0)) for k in range(group)
    ]
    columns = out_weight.shape[1] // n
    steps = jnp.arange(group, dtype=jnp.int32)
    homes = (me // 2 - steps) % group * 2
    dests = jnp.concatenate([homes + (1 - me % 2), homes + me % 2])
    token_attention, weight_rows, token_dq = [], [], []
    for i in halves:
        local_spec = pl.BlockSpec((per_seg, width, QBLK), lambda b, i=i: (b, i, 0))
        home_stats = [stat_slots[i][(group - k) % group] for k in range(group)]
        o_parts = after(last, *o_home[i])
        attention, attention_t = pl.pallas_call(
            functools.partial(attention_kernel, group, heads, i * heads),
            grid=(seg_dev,),
            in_specs=[SMEM, local_spec] + [home_spec] * group + home_specs,
            out_specs=[home_out, pl.BlockSpec((width, seg_len), lambda b: (0, b))],
            out_shape=[home_shape, jax.ShapeDtypeStruct((width, tokens), BF)],
            name="attention",
        )(gating, o_local, *o_parts, *home_stats)
        token_attention.append(exchange(attention.reshape(4, rows, width)))
        if columns % 128:
            weight_rows.append(weight_grad_plain(attention, cot_parts, order))
            continue
        piece = (1, width, columns)
        send, keep = pl.pallas_call(
            weight_grad_kernel,
            grid_spec=pltpu.PrefetchScalarGridSpec(
                num_scalar_prefetch=2,
                grid=(2, group),
                in_specs=[pl.BlockSpec((width, tokens), lambda p, k, *_: (0, 0))]
                + [
                    pl.BlockSpec((rows, columns), lambda p, k, _, to: (0, to[p * group + k]))
                ]
                * 4,
                out_specs=[
                    pl.BlockSpec(piece, lambda p, k, *_: (jnp.where(p == 0, k, group - 1), 0, 0)),
                    pl.BlockSpec(piece, lambda p, k, *_: (jnp.where(p == 0, 0, k), 0, 0)),
                ],
            ),
            out_shape=[jax.ShapeDtypeStruct((group, width, columns), BF)] * 2,
            name="weight_grad",
        )(order, dests, attention_t, *cot_parts)
        got = lax.ppermute(send, "mem", swap)
        sums = [
            (keep[k].astype(F32) + got[k].astype(F32)).astype(BF) for k in range(group)
        ]
        sums = [sums[0]] + [shifted(sums[k], -k) for k in range(1, group)]
        weight_rows.append(functools.reduce(jnp.add, [x.astype(F32) for x in sums]))
    for i in halves:
        local_spec = pl.BlockSpec((per_seg, width, QBLK), lambda b, i=i: (b, i, 0))
        dq = pl.pallas_call(
            functools.partial(query_grad_kernel, group, heads, i * heads),
            grid=(seg_dev,),
            in_specs=[SMEM, local_spec] + [home_spec] * group,
            out_specs=home_out,
            out_shape=home_shape,
            name="query_grad",
        )(gating, dq_local, *dq_home[i])
        token_dq.append(exchange(dq.reshape(4, rows, width)))

    projected = jnp.einsum(
        "stc,scd->td",
        jnp.concatenate(token_attention, axis=2),
        full_weight.reshape(4, full, -1),
        preferred_element_type=F32,
    ).astype(BF)
    dk, dv = after(last, dk, dv)
    return (
        projected,
        side_by_side(jnp.concatenate(token_dq, axis=2)),
        side_by_side(exchange(dk.reshape(4, rows, full))),
        side_by_side(exchange(dv.reshape(4, rows, full))),
        jnp.concatenate(weight_rows, axis=0),
    )


def solution(mesh):
    in_specs = (
        P(("mem", "fsdp"), None),
        P(("mem", "fsdp"), None),
        P(("mem", "fsdp"), None),
        P("mem", "fsdp"),
        P("mem", "fsdp"),
        P(),
        P(),
        P("fsdp", None),
        P(("mem", "fsdp"), None),
    )
    out_specs = (
        P(("mem", "fsdp"), None),
        P(("mem", "fsdp"), None),
        P(("mem", "fsdp"), None),
        P(("mem", "fsdp"), None),
        P("fsdp", "mem"),
    )
    return jax.shard_map(
        per_device, mesh=mesh, in_specs=in_specs, out_specs=out_specs, check_vma=False
    )
```

time: 467 us -> 384 us (0.82)
  the two profiles are of different devices: /device:TPU:0 before, /device:TPU:23 now
where the time goes in v2:
time: 384 us; the launch traced here: 380 us
  waiting for transfers between devices  148 us (39%)
  Pallas kernels  78.8 us (21%)
  starting transfers between devices  67.5 us (18%)
  blocking collectives  33 us (9%)
  local copies, waits for them, and re-layouts  29.5 us (8%)
  between operations  14.3 us (4%)
  other arithmetic  4.48 us (1%)
  matrix products  4.41 us (1%)
    ppermute x18, waiting for transfers between devices, shifted(): return lax.ppermute(x, 'mem', [(i, (i + 2 * k) % n) for i in range(n)])  104 us
    ppermute x18, starting transfers between devices, shifted(): return lax.ppermute(x, 'mem', [(i, (i + 2 * k) % n) for i in range(n)])  38.4 us
    all_to_all x3, blocking collectives, exchange(): return lax.all_to_all(x, 'fsdp', split_axis=0, concat_axis=0, tiled=True)  33 us
    pallas_call x1, Pallas kernels, per_device(): pl.pallas_call(functools.partial(memory_backward, group, pairs, i), grid_...  27.1 us
    pallas_call x1, Pallas kernels, per_device(): pl.pallas_call(functools.partial(memory_forward, group, pairs, i), grid_s...  25.6 us
    all_to_all x4, starting transfers between devices, exchange(): return lax.all_to_all(x, 'fsdp', split_axis=0, concat_axis=0, tiled=True)  23.8 us
    unnamed x79, local copies, waits for them, and re-layouts  23.8 us
    ppermute x1, waiting for transfers between devices, gather_tokens(): far = lax.ppermute(x, 'fsdp', [(i, i ^ 2) for i in range(4)])  21.9 us
  transfers between devices with their start and end apart: 29, of which 15 were waited for; matrix products, arithmetic and copies ran while one was open for 2% of the time, Pallas kernels for 20%

profile of v2, /device:TPU:23, one launch (start us, length us, event | category | flops | bytes accessed | tf_op | source)
XLA Modules:
  0.0 380.0 jit_solution(17218951053317532546)
XLA Ops:
  7.2 1.2 multiply_bitcast_fusion
  8.6 10.4 %all_to_all.35.q_ref.rest_0_ = bf16[4,256,256]{2,1,0:T(8,128)(2,1)S(1)} all-to-all(bf16[4,256,256]{2,1,0:T(8,128)(2,1)S(1)} %bitcast.62), channel_id=1, replica_groups=mesh['mem'=8,'fsdp'=4] {'fsdp'}, dimensions={0} | all-to-all | bytes 1048576 | tf_op jit(solution)/shard_map/all_to_all | solution.py:459
  19.9 1.3 collective-permute-start
  21.2 21.9 %collective-permute-done.1.rest_2_ = bf16[256,2048]{1,0:T(8,128)(2,1)S(1)} collective-permute-done((bf16[256,2048]{1,0:T(8,128)(2,1)S(1)}, bf16[256,2048]{1,0:T(8,128)(2,1)S(1)}, u32[]{:S(2)}, u32[]{:S(2)}) %collective-permute-start.1) | collective-permute-done | bytes 1048608 | tf_op jit(solution)/shard_map/ppermute | solution.py:410
  43.1 1.4 collective-permute-start.2
  44.6 2.4 collective-permute-done.2.rest_3_
  47.0 1.2 copy-done.5
  48.2 2.9 attention_grad.1.rest_0_.rest_4_
  52.2 11.4 %all_to_all.36 = bf16[4,256,256]{2,1,0:T(8,128)(2,1)} all-to-all(bf16[4,256,256]{2,1,0:T(8,128)(2,1)S(1)} %bitcast.63), channel_id=1, replica_groups=mesh['mem'=8,'fsdp'=4] {'fsdp'}, dimensions={0} | all-to-all | bytes 1048576 | tf_op jit(solution)/shard_map/all_to_all | solution.py:459
  63.9 1.2 collective-permute-start.4
  66.1 1.3 collective-permute-start.5
  67.5 1.2 collective-permute-start.7
  69.1 9.5 %collective-permute-done.5.rest_1_ = bf16[4,256,256]{2,1,0:T(8,128)(2,1)S(1)} collective-permute-done((bf16[4,256,256]{2,1,0:T(8,128)(2,1)S(1)}, bf16[4,256,256]{2,1,0:T(8,128)(2,1)S(1)}, u32[]{:S(2)}, u32[]{:S(2)}) %collective-permute-start.5) | collective-permute-done | bytes 524320 | tf_op jit(solution)/shard_map/ppermute | solution.py:456
  79.5 21.9 %collective-permute-done.6.rest_2_ = bf16[4,256,256]{2,1,0:T(8,128)(2,1)S(1)} collective-permute-done((bf16[4,256,256]{2,1,0:T(8,128)(2,1)S(1)}, bf16[4,256,256]{2,1,0:T(8,128)(2,1)S(1)}, u32[]{:S(2)}, u32[]{:S(2)}) %collective-permute-start.6) | collective-permute-done | bytes 524320 | tf_op jit(solution)/shard_map/ppermute | solution.py:456
  102.2 23.1 %collective-permute-start.8 = (bf16[4,256,256]{2,1,0:T(8,128)(2,1)S(1)}, bf16[4,256,256]{2,1,0:T(8,128)(2,1)}, u32[]{:S(2)}, u32[]{:S(2)}) collective-permute-start(bf16[4,256,256]{2,1,0:T(8,128)(2,1)S(1)} %attention_grad.1.rest_0_.rest_4_), channel_id=1, source_target_pairs={{0,8},{4,12},{8,16},{12,20},{16,24},{20,28},{24,0},{28,4},{1,9},{5... | collective-permute-start | bytes 1572872 | tf_op jit(solution)/shard_map/ppermute | solution.py:456
  126.5 1.9 copy.50
  128.4 8.1 %all-to-all-start.1 = ((bf16[4,256,256]{2,1,0:T(8,128)(2,1)}), bf16[4,256,256]{2,1,0:T(8,128)(2,1)}, u32[]{:S(2)}, u32[]{:S(2)}) async-start(bf16[4,256,256]{2,1,0:T(8,128)(2,1)} %bitcast.60), calls=%async_computation.1 | async-start | bytes 1048576 | tf_op jit(solution)/shard_map/all_to_all | solution.py:459
  137.0 18.3 %collective-permute-done.4.v_par = bf16[4096,256]{1,0:T(8,128)(2,1)} collective-permute-done((bf16[4096,256]{1,0:T(8,128)(2,1)}, bf16[4096,256]{1,0:T(8,128)(2,1)}, u32[]{:S(2)}, u32[]{:S(2)}) %collective-permute-start.4) | collective-permute-done | bytes 2097184 | tf_op jit(solution)/shard_map/ppermute | solution.py:473
  155.3 3.9 %collective-permute-done.9.rest_6_ = bf16[4,256,256]{2,1,0:T(8,128)(2,1)} collective-permute-done((bf16[4,256,256]{2,1,0:T(8,128)(2,1)S(1)}, bf16[4,256,256]{2,1,0:T(8,128)(2,1)}, u32[]{:S(2)}, u32[]{:S(2)}) %collective-permute-start.9) | collective-permute-done | bytes 524320 | tf_op jit(solution)/shard_map/ppermute | solution.py:456
  159.2 1.6 copy-done.1
  161.8 1.0 copy-done.11
  162.8 1.0 copy-done.14
  163.9 25.6 %memory_forward.1 = (bf16[8,256,128]{2,1,0:T(8,128)(2,1)S(1)}, bf16[8,256,128]{2,1,0:T(8,128)(2,1)}, bf16[8,256,128]{2,1,0:T(8,128)(2,1)S(1)}, bf16[8,256,128]{2,1,0:T(8,128)(2,1)S(1)}, f32[4,8,2,512]{3,2,1,0:T(2,128)S(1)}) custom-call(s32[8]{0:T(128)S(1)} %reduce_sum.39.counts, s32[128]{0:T(128)S(1)} %reshape.300.places, s32[128]{0:T(128)S(1)} %add.149.homes, ...), custom_call_target="tpu_custom_call" | custom-call | tf_op jit(solution)/shard_map/memory_forward/pallas_call | solution.py:542
  191.9 1.5 collective-permute-start.11
  193.4 1.2 collective-permute-start.13
  195.3 1.2 copy-done.6
  196.5 9.2 %local.1 = (f32[8,256,128]{2,1,0:T(8,128)S(1)}, f32[8,256,128]{2,1,0:T(8,128)S(1)}, bf16[1024,256]{1,0:T(8,128)(2,1)S(1)}, bf16[1024,256]{1,0:T(8,128)(2,1)S(1)}) custom-call(f32[4]{0:T(128)S(1)} %add_divide_fusion.gate, bf16[4,256,256]{2,1,0:T(8,128)(2,1)S(1)} %all_to_all.35.q_ref.rest_0_, bf16[1024,256]{1,0:T(8,128)(2,1)} %bitcast.3.k_ref, ...), custom_call_target="tpu_custom_call" | custom-call | tf_op jit(solution)/shard_map/local/pallas_call | solution.py:504
  209.3 1.9 collective-permute-done.12.rest_10_.rest_6_
  211.2 3.3 collective-permute-done.13.rest_11_.rest_5_
  214.5 1.0 copy-done.9
  217.6 27.1 %memory_backward.1 = (bf16[8,256,128]{2,1,0:T(8,128)(2,1)S(1)}, bf16[8,256,128]{2,1,0:T(8,128)(2,1)S(1)}, bf16[8,256,128]{2,1,0:T(8,128)(2,1)S(1)}, bf16[8,256,128]{2,1,0:T(8,128)(2,1)S(1)}) custom-call(s32[8]{0:T(128)S(1)} %reduce_sum.39.counts, s32[128]{0:T(128)S(1)} %reshape.300.places, s32[128]{0:T(128)S(1)} %add.149.homes, ...), custom_call_target="tpu_custom_call" | custom-call | tf_op jit(solution)/shard_map/memory_backward/pallas_call | solution.py:564
  248.0 4.9 %all-to-all-start.5 = ((bf16[4,256,256]{2,1,0:T(8,128)(2,1)}), bf16[4,256,256]{2,1,0:T(8,128)(2,1)S(1)}, u32[]{:S(2)}, u32[]{:S(2)}) async-start(bf16[4,256,256]{2,1,0:T(8,128)(2,1)} %bitcast.57), calls=%async_computation.5 | async-start | bytes 1048576 | tf_op jit(solution)/shard_map/all_to_all | solution.py:459
  254.4 4.2 %collective-permute-start.18 = (bf16[8,256,128]{2,1,0:T(8,128)(2,1)}, bf16[8,256,128]{2,1,0:T(8,128)(2,1)S(1)}, u32[]{:S(2)}, u32[]{:S(2)}) collective-permute-start(bf16[8,256,128]{2,1,0:T(8,128)(2,1)} %copy-done.30), channel_id=1, source_target_pairs={{0,16},{4,20},{8,24},{12,28},{16,0},{20,4},{24,8},{28,12},{1,17},{... | collective-permute-start | bytes 1572872 | tf_op jit(solution)/shard_map/ppermute | solution.py:456
  258.6 1.3 all-to-all-done.5
  259.9 5.3 %all-to-all-start.6 = ((bf16[4,256,256]{2,1,0:T(8,128)(2,1)}), bf16[4,256,256]{2,1,0:T(8,128)(2,1)S(1)}, u32[]{:S(2)}, u32[]{:S(2)}) async-start(bf16[4,256,256]{2,1,0:T(8,128)(2,1)} %bitcast.56), calls=%async_computation.6 | async-start | bytes 1048576 | tf_op jit(solution)/shard_map/all_to_all | solution.py:459
  265.9 21.1 %collective-permute-done.15.rest_2_ = bf16[8,256,128]{2,1,0:T(8,128)(2,1)S(1)} collective-permute-done((bf16[8,256,128]{2,1,0:T(8,128)(2,1)}, bf16[8,256,128]{2,1,0:T(8,128)(2,1)S(1)}, u32[]{:S(2)}, u32[]{:S(2)}) %collective-permute-start.15) | collective-permute-done | bytes 524320 | tf_op jit(solution)/shard_map/ppermute | solution.py:456
  287.1 22.9 %collective-permute-done.16.rest_3_ = bf16[8,256,128]{2,1,0:T(8,128)(2,1)} collective-permute-done((bf16[8,256,128]{2,1,0:T(8,128)(2,1)}, bf16[8,256,128]{2,1,0:T(8,128)(2,1)}, u32[]{:S(2)}, u32[]{:S(2)}) %collective-permute-start.16) | collective-permute-done | bytes 524320 | tf_op jit(solution)/shard_map/ppermute | solution.py:456
  310.0 3.0 attention.1
  313.0 8.1 %weight_grad.1 = (bf16[4,256,256]{2,1,0:T(8,128)(2,1)}, bf16[4,256,256]{2,1,0:T(8,128)(2,1)}) custom-call(s32[4]{0:T(128)} %copy-done.26, s32[8]{0:T(128)} %pad_add_fusion.dests, bf16[256,1024]{1,0:T(8,128)(2,1)} %get-tuple-element.64.attention_ref, bf16[256,2048]{1,0:T(8,128)(2,1)} %rest_0_.1, bf16[256,2048]{1,0:T(8,128)(2,1)} %collective-permute-done.rest_1_, ...), custom_call_target="tpu_custom_call" | custom-call | tf_op jit(solution)/shard_map/weight_grad/pallas_call | solution.py:611
  321.2 10.8 %collective-permute-done.18.rest_2_ = bf16[8,256,128]{2,1,0:T(8,128)(2,1)S(1)} collective-permute-done((bf16[8,256,128]{2,1,0:T(8,128)(2,1)}, bf16[8,256,128]{2,1,0:T(8,128)(2,1)S(1)}, u32[]{:S(2)}, u32[]{:S(2)}) %collective-permute-start.18) | collective-permute-done | bytes 524320 | tf_op jit(solution)/shard_map/ppermute | solution.py:456
  333.2 2.8 query_grad.1
  336.0 11.2 %all_to_all.37 = bf16[4,256,256]{2,1,0:T(8,128)(2,1)S(1)} all-to-all(bf16[4,256,256]{2,1,0:T(8,128)(2,1)} %bitcast.64), channel_id=1, replica_groups=mesh['mem'=8,'fsdp'=4] {'fsdp'}, dimensions={0} | all-to-all | bytes 1048576 | tf_op jit(solution)/shard_map/all_to_all | solution.py:459
  347.2 5.4 %all-to-all-start.3 = ((bf16[4,256,256]{2,1,0:T(8,128)(2,1)}), bf16[4,256,256]{2,1,0:T(8,128)(2,1)S(1)}, u32[]{:S(2)}, u32[]{:S(2)}) async-start(bf16[4,256,256]{2,1,0:T(8,128)(2,1)} %bitcast.9), calls=%async_computation.3 | async-start | bytes 1048576 | tf_op jit(solution)/shard_map/all_to_all | solution.py:459
  352.7 2.9 collective-permute-start.22
  355.6 1.4 collective-permute-start.23
  359.6 4.2 %collective-permute-done.22 = bf16[256,256]{1,0:T(8,128)(2,1)S(1)} collective-permute-done((bf16[256,256]{1,0:T(8,128)(2,1)S(1)}, bf16[256,256]{1,0:T(8,128)(2,1)S(1)}, u32[]{:S(2)}, u32[]{:S(2)}) %collective-permute-start.22) | collective-permute-done | bytes 131104 | tf_op jit(solution)/shard_map/ppermute | solution.py:456
  363.8 4.1 %collective-permute-done.23 = bf16[256,256]{1,0:T(8,128)(2,1)S(1)} collective-permute-done((bf16[256,256]{1,0:T(8,128)(2,1)S(1)}, bf16[256,256]{1,0:T(8,128)(2,1)S(1)}, u32[]{:S(2)}, u32[]{:S(2)}) %collective-permute-start.23) | collective-permute-done | bytes 131104 | tf_op jit(solution)/shard_map/ppermute | solution.py:456
  368.7 4.4 %fusion = bf16[256,2048]{1,0:T(8,128)(2,1)} fusion(bf16[4,256,256]{2,1,0:T(8,128)(2,1)S(1)} %all-to-all-done.3, bf16[4,256,2048]{2,1,0:T(8,128)(2,1)} %bitcast.72), kind=kOutput, calls=%fused_computation.2 | convolution fusion | flops 1074266112 | bytes 5767168 | tf_op jit(solution)/shard_map/stc,scd->td/dot_general | solution.py:647
  (133 shorter events, 27.2 us)
Async XLA Ops:
  7.2 11.8 %copy-start.3 = (bf16[256,2048]{1,0:T(8,128)(2,1)S(1)}, bf16[256,2048]{1,0:T(8,128)(2,1)}, u32[]{:S(2)}) copy-start(bf16[256,2048]{1,0:T(8,128)(2,1)} %rest_0_.1) | copy-start | bytes 3145732
  7.2 361.6 %all-gather.2.cloned.1.call-start = ((), (), s32[]{:S(2)}) async-start(), calls=%async_computation.7 | async-start | bytes 5242880 | tf_op jit(solution)/shard_map/all_gather | solution.py:496
  19.0 24.1 %collective-permute-start.1 = (bf16[256,2048]{1,0:T(8,128)(2,1)S(1)}, bf16[256,2048]{1,0:T(8,128)(2,1)S(1)}, u32[]{:S(2)}, u32[]{:S(2)}) collective-permute-start(bf16[256,2048]{1,0:T(8,128)(2,1)S(1)} %copy-done.3), channel_id=1, source_target_pairs={{0,2},{1,3},{2,0},{3,1},{4,6},{5,7},{6,4},{7,5},{8,10},{9,11},{10,... | collective-permute-start | bytes 3145736 | tf_op jit(solution)/shard_map/ppermute | solution.py:410
  19.9 24.7 %collective-permute-start = (bf16[256,2048]{1,0:T(8,128)(2,1)S(1)}, bf16[256,2048]{1,0:T(8,128)(2,1)}, u32[]{:S(2)}, u32[]{:S(2)}) collective-permute-start(bf16[256,2048]{1,0:T(8,128)(2,1)S(1)} %copy-done.3), channel_id=1, source_target_pairs={{0,1},{1,0},{2,3},{3,2},{4,5},{5,4},{6,7},{7,6},{8,9},{9,8},{10,11... | collective-permute-start | bytes 3145736 | tf_op jit(solution)/shard_map/ppermute | solution.py:411
  43.1 3.9 %collective-permute-start.2 = (bf16[256,2048]{1,0:T(8,128)(2,1)S(1)}, bf16[256,2048]{1,0:T(8,128)(2,1)}, u32[]{:S(2)}, u32[]{:S(2)}) collective-permute-start(bf16[256,2048]{1,0:T(8,128)(2,1)S(1)} %collective-permute-done.1.rest_2_), channel_id=1, source_target_pairs={{0,1},{1,0},{2,3},{3,2},{4,5},{5,4},{6,7},{7,6},{8,9},{9,8},{10,11... | collective-permute-start | bytes 3145736 | tf_op jit(solution)/shard_map/ppermute | solution.py:412
  44.6 6.6 %copy-start.26 = (s32[4]{0:T(128)}, s32[4]{0:T(128)S(1)}, u32[]{:S(2)}) copy-start(s32[4]{0:T(128)S(1)} %iota_xor_fusion.order) | copy-start | bytes 52
  47.0 1.2 copy-start.5
  48.2 4.0 %copy-start.32 = (bf16[256,1024]{1,0:T(8,128)(2,1)S(1)}, bf16[256,1024]{1,0:T(8,128)(2,1)}, u32[]{:S(2)}) copy-start(bf16[256,1024]{1,0:T(8,128)(2,1)} %param.11) | copy-start | bytes 1572868
  52.2 11.4 %copy-start = (bf16[4096,256]{1,0:T(8,128)(2,1)S(1)}, bf16[4096,256]{1,0:T(8,128)(2,1)}, u32[]{:S(2)}) copy-start(bf16[4096,256]{1,0:T(8,128)(2,1)} %k_own.3) | copy-start | bytes 6291460
  52.2 13.0 %copy-start.38 = (s32[16,4,8]{0,2,1:T(8,128)S(1)}, s32[16,4,8]{0,2,1:T(8,128)}, u32[]{:S(2)}) copy-start(s32[16,4,8]{0,2,1:T(8,128)} %param.14) | copy-start | bytes 6148
  63.6 73.4 %collective-permute-start.3 = (bf16[4096,256]{1,0:T(8,128)(2,1)S(1)}, bf16[4096,256]{1,0:T(8,128)(2,1)}, u32[]{:S(2)}, u32[]{:S(2)}) collective-permute-start(bf16[4096,256]{1,0:T(8,128)(2,1)S(1)} %copy-done), channel_id=1, source_target_pairs={{0,4},{4,0},{8,12},{12,8},{16,20},{20,16},{24,28},{28,24},{1,5},{5... | collective-permute-start | bytes 6291464 | tf_op jit(solution)/shard_map/ppermute | solution.py:472
  63.9 91.4 %collective-permute-start.4 = (bf16[4096,256]{1,0:T(8,128)(2,1)}, bf16[4096,256]{1,0:T(8,128)(2,1)}, u32[]{:S(2)}, u32[]{:S(2)}) collective-permute-start(bf16[4096,256]{1,0:T(8,128)(2,1)} %v_own.3), channel_id=1, source_target_pairs={{0,4},{4,0},{8,12},{12,8},{16,20},{20,16},{24,28},{28,24},{1,5},{5... | collective-permute-start | bytes 6291464 | tf_op jit(solution)/shard_map/ppermute | solution.py:473
  66.1 12.5 %collective-permute-start.5 = (bf16[4,256,256]{2,1,0:T(8,128)(2,1)S(1)}, bf16[4,256,256]{2,1,0:T(8,128)(2,1)S(1)}, u32[]{:S(2)}, u32[]{:S(2)}) collective-permute-start(bf16[4,256,256]{2,1,0:T(8,128)(2,1)S(1)} %all_to_all.35.q_ref.rest_0_), channel_id=1, source_target_pairs={{0,8},{4,12},{8,16},{12,20},{16,24},{20,28},{24,0},{28,4},{1,9},{5... | collective-permute-start | bytes 1572872 | tf_op jit(solution)/shard_map/ppermute | solution.py:456
  67.5 33.9 %collective-permute-start.6 = (bf16[4,256,256]{2,1,0:T(8,128)(2,1)S(1)}, bf16[4,256,256]{2,1,0:T(8,128)(2,1)S(1)}, u32[]{:S(2)}, u32[]{:S(2)}) collective-permute-start(bf16[4,256,256]{2,1,0:T(8,128)(2,1)S(1)} %all_to_all.35.q_ref.rest_0_), channel_id=1, source_target_pairs={{0,16},{4,20},{8,24},{12,28},{16,0},{20,4},{24,8},{28,12},{1,17},{... | collective-permute-start | bytes 1572872 | tf_op jit(solution)/shard_map/ppermute | solution.py:456
  67.5 57.8 %collective-permute-start.7 = (bf16[4,256,256]{2,1,0:T(8,128)(2,1)S(1)}, bf16[4,256,256]{2,1,0:T(8,128)(2,1)S(1)}, u32[]{:S(2)}, u32[]{:S(2)}) collective-permute-start(bf16[4,256,256]{2,1,0:T(8,128)(2,1)S(1)} %all_to_all.35.q_ref.rest_0_), channel_id=1, source_target_pairs={{0,24},{4,28},{8,0},{12,4},{16,8},{20,12},{24,16},{28,20},{1,25},{... | collective-permute-start | bytes 1572872 | tf_op jit(solution)/shard_map/ppermute | solution.py:456
  79.4 75.8 %collective-permute-start.10 = (bf16[4,256,256]{2,1,0:T(8,128)(2,1)S(1)}, bf16[4,256,256]{2,1,0:T(8,128)(2,1)}, u32[]{:S(2)}, u32[]{:S(2)}) collective-permute-start(bf16[4,256,256]{2,1,0:T(8,128)(2,1)S(1)} %attention_grad.1.rest_0_.rest_4_), channel_id=1, source_target_pairs={{0,24},{4,28},{8,0},{12,4},{16,8},{20,12},{24,16},{28,20},{1,25},{... | collective-permute-start | bytes 1572872 | tf_op jit(solution)/shard_map/ppermute | solution.py:456
  102.2 53.1 %collective-permute-start.8 = (bf16[4,256,256]{2,1,0:T(8,128)(2,1)S(1)}, bf16[4,256,256]{2,1,0:T(8,128)(2,1)}, u32[]{:S(2)}, u32[]{:S(2)}) collective-permute-start(bf16[4,256,256]{2,1,0:T(8,128)(2,1)S(1)} %attention_grad.1.rest_0_.rest_4_), channel_id=1, source_target_pairs={{0,8},{4,12},{8,16},{12,20},{16,24},{20,28},{24,0},{28,4},{1,9},{5... | collective-permute-start | bytes 1572872 | tf_op jit(solution)/shard_map/ppermute | solution.py:456
  126.1 33.0 %collective-permute-start.9 = (bf16[4,256,256]{2,1,0:T(8,128)(2,1)S(1)}, bf16[4,256,256]{2,1,0:T(8,128)(2,1)}, u32[]{:S(2)}, u32[]{:S(2)}) collective-permute-start(bf16[4,256,256]{2,1,0:T(8,128)(2,1)S(1)} %attention_grad.1.rest_0_.rest_4_), channel_id=1, source_target_pairs={{0,16},{4,20},{8,24},{12,28},{16,0},{20,4},{24,8},{28,12},{1,17},{... | collective-permute-start | bytes 1572872 | tf_op jit(solution)/shard_map/ppermute | solution.py:456
  128.4 67.0 %all-to-all-start.1 = ((bf16[4,256,256]{2,1,0:T(8,128)(2,1)}), bf16[4,256,256]{2,1,0:T(8,128)(2,1)}, u32[]{:S(2)}, u32[]{:S(2)}) async-start(bf16[4,256,256]{2,1,0:T(8,128)(2,1)} %bitcast.60), calls=%async_computation.1 | async-start | bytes 1048576 | tf_op jit(solution)/shard_map/all_to_all | solution.py:459
  159.2 1.6 copy-start.1
  191.9 52.8 %copy-start.18 = (f32[4,8,2,512]{3,2,1,0:T(2,128)}, f32[4,8,2,512]{3,2,1,0:T(2,128)S(1)}, u32[]{:S(2)}) copy-start(f32[4,8,2,512]{3,2,1,0:T(2,128)S(1)} %get-tuple-element.41.rest_8_.rest_4_) | copy-start | bytes 393220
  191.9 66.7 %collective-permute-start.14 = (bf16[8,256,128]{2,1,0:T(8,128)(2,1)}, bf16[8,256,128]{2,1,0:T(8,128)(2,1)}, u32[]{:S(2)}, u32[]{:S(2)}) collective-permute-start(bf16[8,256,128]{2,1,0:T(8,128)(2,1)} %get-tuple-element.47), channel_id=1, source_target_pairs={{0,24},{4,28},{8,0},{12,4},{16,8},{20,12},{24,16},{28,20},{1,25},{... | collective-permute-start | bytes 1572872 | tf_op jit(solution)/shard_map/ppermute | solution.py:456
  191.9 17.4 %collective-permute-start.11 = (f32[4,8,2,512]{3,2,1,0:T(2,128)S(1)}, f32[4,8,2,512]{3,2,1,0:T(2,128)S(1)}, u32[]{:S(2)}, u32[]{:S(2)}) collective-permute-start(f32[4,8,2,512]{3,2,1,0:T(2,128)S(1)} %get-tuple-element.41.rest_8_.rest_4_), channel_id=1, source_target_pairs={{0,8},{4,12},{8,16},{12,20},{16,24},{20,28},{24,0},{28,4},{1,9},{5... | collective-permute-start | bytes 393224 | tf_op jit(solution)/shard_map/ppermute | solution.py:456
  193.4 17.8 %collective-permute-start.12 = (f32[4,8,2,512]{3,2,1,0:T(2,128)S(1)}, f32[4,8,2,512]{3,2,1,0:T(2,128)S(1)}, u32[]{:S(2)}, u32[]{:S(2)}) collective-permute-start(f32[4,8,2,512]{3,2,1,0:T(2,128)S(1)} %get-tuple-element.41.rest_8_.rest_4_), channel_id=1, source_target_pairs={{0,16},{4,20},{8,24},{12,28},{16,0},{20,4},{24,8},{28,12},{1,17},{... | collective-permute-start | bytes 393224 | tf_op jit(solution)/shard_map/ppermute | solution.py:456
  193.4 21.1 %collective-permute-start.13 = (f32[4,8,2,512]{3,2,1,0:T(2,128)S(1)}, f32[4,8,2,512]{3,2,1,0:T(2,128)}, u32[]{:S(2)}, u32[]{:S(2)}) collective-permute-start(f32[4,8,2,512]{3,2,1,0:T(2,128)S(1)} %get-tuple-element.41.rest_8_.rest_4_), channel_id=1, source_target_pairs={{0,24},{4,28},{8,0},{12,4},{16,8},{20,12},{24,16},{28,20},{1,25},{... | collective-permute-start | bytes 393224 | tf_op jit(solution)/shard_map/ppermute | solution.py:456
  195.3 49.5 %copy-start.25 = (f32[4]{0:T(128)}, f32[4]{0:T(128)S(1)}, u32[]{:S(2)}) copy-start(f32[4]{0:T(128)S(1)} %add_divide_fusion.gate) | copy-start | bytes 52
  195.3 19.2 %copy-start.2 = (bf16[4096,256]{1,0:T(8,128)(2,1)S(1)}, bf16[4096,256]{1,0:T(8,128)(2,1)}, u32[]{:S(2)}) copy-start(bf16[4096,256]{1,0:T(8,128)(2,1)} %v_own.3) | copy-start | bytes 6291460
  195.3 1.2 copy-start.6
  205.7 1.0 copy-start.16
  209.3 35.5 %copy-start.19 = (f32[4,8,2,512]{3,2,1,0:T(2,128)}, f32[4,8,2,512]{3,2,1,0:T(2,128)S(1)}, u32[]{:S(2)}) copy-start(f32[4,8,2,512]{3,2,1,0:T(2,128)S(1)} %collective-permute-done.11.rest_9_.rest_7_) | copy-start | bytes 393220
  211.2 33.6 %copy-start.20 = (f32[4,8,2,512]{3,2,1,0:T(2,128)}, f32[4,8,2,512]{3,2,1,0:T(2,128)S(1)}, u32[]{:S(2)}) copy-start(f32[4,8,2,512]{3,2,1,0:T(2,128)S(1)} %collective-permute-done.12.rest_10_.rest_6_) | copy-start | bytes 393220
  214.5 1.0 copy-start.9
  248.0 11.9 %all-to-all-start.5 = ((bf16[4,256,256]{2,1,0:T(8,128)(2,1)}), bf16[4,256,256]{2,1,0:T(8,128)(2,1)S(1)}, u32[]{:S(2)}, u32[]{:S(2)}) async-start(bf16[4,256,256]{2,1,0:T(8,128)(2,1)} %bitcast.57), calls=%async_computation.5 | async-start | bytes 1048576 | tf_op jit(solution)/shard_map/all_to_all | solution.py:459
  253.0 34.1 %collective-permute-start.15 = (bf16[8,256,128]{2,1,0:T(8,128)(2,1)}, bf16[8,256,128]{2,1,0:T(8,128)(2,1)S(1)}, u32[]{:S(2)}, u32[]{:S(2)}) collective-permute-start(bf16[8,256,128]{2,1,0:T(8,128)(2,1)} %copy-done.28), channel_id=1, source_target_pairs={{0,16},{4,20},{8,24},{12,28},{16,0},{20,4},{24,8},{28,12},{1,17},{... | collective-permute-start | bytes 1572872 | tf_op jit(solution)/shard_map/ppermute | solution.py:456
  253.0 57.0 %collective-permute-start.16 = (bf16[8,256,128]{2,1,0:T(8,128)(2,1)}, bf16[8,256,128]{2,1,0:T(8,128)(2,1)}, u32[]{:S(2)}, u32[]{:S(2)}) collective-permute-start(bf16[8,256,128]{2,1,0:T(8,128)(2,1)} %copy-done.27), channel_id=1, source_target_pairs={{0,8},{4,12},{8,16},{12,20},{16,24},{20,28},{24,0},{28,4},{1,9},{5... | collective-permute-start | bytes 1572872 | tf_op jit(solution)/shard_map/ppermute | solution.py:456
  253.9 67.3 %collective-permute-start.17 = (bf16[8,256,128]{2,1,0:T(8,128)(2,1)}, bf16[8,256,128]{2,1,0:T(8,128)(2,1)S(1)}, u32[]{:S(2)}, u32[]{:S(2)}) collective-permute-start(bf16[8,256,128]{2,1,0:T(8,128)(2,1)} %copy-done.31), channel_id=1, source_target_pairs={{0,24},{4,28},{8,0},{12,4},{16,8},{20,12},{24,16},{28,20},{1,25},{... | collective-permute-start | bytes 1572872 | tf_op jit(solution)/shard_map/ppermute | solution.py:456
  254.4 77.6 %collective-permute-start.18 = (bf16[8,256,128]{2,1,0:T(8,128)(2,1)}, bf16[8,256,128]{2,1,0:T(8,128)(2,1)S(1)}, u32[]{:S(2)}, u32[]{:S(2)}) collective-permute-start(bf16[8,256,128]{2,1,0:T(8,128)(2,1)} %copy-done.30), channel_id=1, source_target_pairs={{0,16},{4,20},{8,24},{12,28},{16,0},{20,4},{24,8},{28,12},{1,17},{... | collective-permute-start | bytes 1572872 | tf_op jit(solution)/shard_map/ppermute | solution.py:456
  258.6 73.8 %collective-permute-start.19 = (bf16[8,256,128]{2,1,0:T(8,128)(2,1)}, bf16[8,256,128]{2,1,0:T(8,128)(2,1)S(1)}, u32[]{:S(2)}, u32[]{:S(2)}) collective-permute-start(bf16[8,256,128]{2,1,0:T(8,128)(2,1)} %copy-done.29), channel_id=1, source_target_pairs={{0,8},{4,12},{8,16},{12,20},{16,24},{20,28},{24,0},{28,4},{1,9},{5... | collective-permute-start | bytes 1572872 | tf_op jit(solution)/shard_map/ppermute | solution.py:456
  259.9 76.1 %all-to-all-start.6 = ((bf16[4,256,256]{2,1,0:T(8,128)(2,1)}), bf16[4,256,256]{2,1,0:T(8,128)(2,1)S(1)}, u32[]{:S(2)}, u32[]{:S(2)}) async-start(bf16[4,256,256]{2,1,0:T(8,128)(2,1)} %bitcast.56), calls=%async_computation.6 | async-start | bytes 1048576 | tf_op jit(solution)/shard_map/all_to_all | solution.py:459
  287.1 22.9 %copy-start.37 = (bf16[8,256,128]{2,1,0:T(8,128)(2,1)}, bf16[8,256,128]{2,1,0:T(8,128)(2,1)S(1)}, u32[]{:S(2)}) copy-start(bf16[8,256,128]{2,1,0:T(8,128)(2,1)S(1)} %collective-permute-done.15.rest_2_) | copy-start | bytes 1572868
  321.2 31.4 %collective-permute-start.20 = (bf16[4,256,256]{2,1,0:T(8,128)(2,1)}, bf16[4,256,256]{2,1,0:T(8,128)(2,1)S(1)}, u32[]{:S(2)}, u32[]{:S(2)}) collective-permute-start(bf16[4,256,256]{2,1,0:T(8,128)(2,1)} %get-tuple-element.66), channel_id=1, source_target_pairs={{0,4},{4,0},{8,12},{12,8},{16,20},{20,16},{24,28},{28,24},{1,5},{5... | collective-permute-start | bytes 1572872 | tf_op jit(solution)/shard_map/ppermute | solution.py:629
  321.2 12.0 %copy-start.34 = (bf16[8,256,128]{2,1,0:T(8,128)(2,1)}, bf16[8,256,128]{2,1,0:T(8,128)(2,1)S(1)}, u32[]{:S(2)}) copy-start(bf16[8,256,128]{2,1,0:T(8,128)(2,1)S(1)} %collective-permute-done.17.rest_1_) | copy-start | bytes 1572868
  332.0 1.1 copy-start.35
  333.2 19.4 %copy-start.33 = (bf16[4,256,256]{2,1,0:T(8,128)(2,1)S(1)}, bf16[4,256,256]{2,1,0:T(8,128)(2,1)}, u32[]{:S(2)}) copy-start(bf16[4,256,256]{2,1,0:T(8,128)(2,1)} %get-tuple-element.65) | copy-start | bytes 1572868
  347.2 21.5 %all-to-all-start.3 = ((bf16[4,256,256]{2,1,0:T(8,128)(2,1)}), bf16[4,256,256]{2,1,0:T(8,128)(2,1)S(1)}, u32[]{:S(2)}, u32[]{:S(2)}) async-start(bf16[4,256,256]{2,1,0:T(8,128)(2,1)} %bitcast.9), calls=%async_computation.3 | async-start | bytes 1048576 | tf_op jit(solution)/shard_map/all_to_all | solution.py:459
  352.7 6.9 %collective-permute-start.21 = (bf16[256,256]{1,0:T(8,128)(2,1)S(1)}, bf16[256,256]{1,0:T(8,128)(2,1)S(1)}, u32[]{:S(2)}, u32[]{:S(2)}) collective-permute-start(bf16[256,256]{1,0:T(8,128)(2,1)S(1)} %get-tuple-element.69), channel_id=1, source_target_pairs={{0,24},{4,28},{8,0},{12,4},{16,8},{20,12},{24,16},{28,20},{1,25},{... | collective-permute-start | bytes 393224 | tf_op jit(solution)/shard_map/ppermute | solution.py:456
  352.7 11.1 %collective-permute-start.22 = (bf16[256,256]{1,0:T(8,128)(2,1)S(1)}, bf16[256,256]{1,0:T(8,128)(2,1)S(1)}, u32[]{:S(2)}, u32[]{:S(2)}) collective-permute-start(bf16[256,256]{1,0:T(8,128)(2,1)S(1)} %get-tuple-element.71), channel_id=1, source_target_pairs={{0,16},{4,20},{8,24},{12,28},{16,0},{20,4},{24,8},{28,12},{1,17},{... | collective-permute-start | bytes 393224 | tf_op jit(solution)/shard_map/ppermute | solution.py:456
  355.6 12.3 %collective-permute-start.23 = (bf16[256,256]{1,0:T(8,128)(2,1)S(1)}, bf16[256,256]{1,0:T(8,128)(2,1)S(1)}, u32[]{:S(2)}, u32[]{:S(2)}) collective-permute-start(bf16[256,256]{1,0:T(8,128)(2,1)S(1)} %get-tuple-element.70), channel_id=1, source_target_pairs={{0,8},{4,12},{8,16},{12,20},{16,24},{20,28},{24,0},{28,4},{1,9},{5... | collective-permute-start | bytes 393224 | tf_op jit(solution)/shard_map/ppermute | solution.py:456
  (20 other events, 17.6 us)
Sparse Core Ops, SparseCore 0:
  63.7 35.1 all-gather.1
